TPU v7x, 32 devices: a whole 2x2x4 slice. The times are simulated.
32 devices in a mesh: group: 4 (over y, x), dom: 8 (over z, core).
Axes of the slice: x: 2, y: 2, z: 4, core: 2. Of those that a mesh axis runs over, the one named last changes fastest.
Arguments:
- node_lat: bfloat16 [65536, 256], P(('group', 'dom')), may hold values from -6 to 6
- edge_lat: bfloat16 [262144, 256], P(('group', 'dom')), may hold values from -6 to 6
- edge_send: int32 [262144], P(('group', 'dom')), may hold values from 0 to 3071, as said below
- halo_list: int32 [32768], P(('group', 'dom')), may hold values from 0 to 2047
- pool_id: int32 [65536], P(('group', 'dom')), may hold values from 0 to 1023
- coarse_lat: bfloat16 [8192, 256], P(('group', 'dom')), may hold values from -6 to 6
- cedge_lat: bfloat16 [32768, 256], P(('group', 'dom')), may hold values from -6 to 6
- cedge_send: int32 [32768], P(('group', 'dom')), may hold values from 0 to 511, as said below
- chalo_list: int32 [8192], P(('group', 'dom')), may hold values from 0 to 255
- fine_edge_in: bfloat16 [3, 256, 256], replicated, may hold values from -0.21875 to 0.21875
- fine_edge_out: bfloat16 [256, 256], replicated, may hold values from -0.375 to 0.375
- fine_node_in: bfloat16 [2, 256, 256], replicated, may hold values from -0.25 to 0.25
- fine_node_out: bfloat16 [256, 256], replicated, may hold values from -0.375 to 0.375
- fine_bias: float32 [4, 256], replicated, may hold values from -3 to 3
- fine_gain: float32 [2, 256], replicated, may hold values from 0.1 to 1.9
- coarse_edge_in: bfloat16 [3, 256, 256], replicated, may hold values from -0.21875 to 0.21875
- coarse_edge_out: bfloat16 [256, 256], replicated, may hold values from -0.375 to 0.375
- coarse_node_in: bfloat16 [2, 256, 256], replicated, may hold values from -0.25 to 0.25
- coarse_node_out: bfloat16 [256, 256], replicated, may hold values from -0.375 to 0.375
- coarse_bias: float32 [4, 256], replicated, may hold values from -3 to 3
- coarse_gain: float32 [2, 256], replicated, may hold values from 0.1 to 1.9
Outputs:
- fine_out: bfloat16 [65536, 256], P(('group', 'dom'))
- coarse_out: bfloat16 [8192, 256], P(('group', 'dom'))
Inputs may be any that keep to these rules, and one draw needn't show every extreme that they name: `edge_send`: indices into the block's extended rows: below 512 the lower neighbour's rows, from 2560 on the upper neighbour's; a block never names the rows of a neighbour it lacks. `cedge_send`: indices into the block's extended coarse rows: below 128 the lower neighbour's rows, from 384 on the upper neighbour's; a block never names the rows of a neighbour it lacks.
All inputs are finite; a program needn't handle non-finite values.
Results may differ from a plain program's by a relative error of at most 0.012.
Values may be sent and summed in bfloat16 or wider, within the bound.
A program may use at most 128 MiB of HBM per device.

v0:
```python
import jax
import jax.numpy as jnp
from jax import lax
from jax.sharding import PartitionSpec as P

EPSILON = 1e-05


def padded(block, sides, width):
    for axis, dim in sides:
        count = lax.axis_size(axis)
        forward = [(i, i + 1) for i in range(count - 1)]
        backward = [(target, source) for source, target in forward]
        low = lax.ppermute(
            lax.slice_in_dim(block, block.shape[dim] - width, None, axis=dim), axis, forward
        )
        high = lax.ppermute(lax.slice_in_dim(block, 0, width, axis=dim), axis, backward)
        block = jnp.concatenate([low, block, high], axis=dim)
    return block


def layer_norm_rows(values):
    row_mean = jnp.mean(values, axis=-1, keepdims=True)
    centred = values - row_mean
    variance = jnp.mean(centred * centred, axis=-1, keepdims=True)
    return centred * lax.rsqrt(variance + EPSILON)


def edge_node(
    sender_proj, own_rows, edge_rows, senders, edge_in, edge_out, node_in, node_out, biases, gains
):
    node_count = own_rows.shape[0]
    width = own_rows.shape[1]
    fanin = edge_rows.shape[0] // node_count
    receiver_proj = jnp.dot(own_rows, edge_in[1], preferred_element_type=jnp.float32)
    edge_pre = jnp.dot(edge_rows, edge_in[2], preferred_element_type=jnp.float32)
    edge_pre = edge_pre + sender_proj[senders].astype(jnp.float32) + biases[0]
    edge_pre = (edge_pre.reshape(node_count, fanin, width) + receiver_proj[:, None, :]).reshape(
        node_count * fanin, width
    )
    edge_hidden = jnp.maximum(edge_pre, 0.0).astype(jnp.bfloat16)
    message = (
        layer_norm_rows(
            jnp.dot(edge_hidden, edge_out, preferred_element_type=jnp.float32) + biases[1]
        )
        * gains[0]
    )
    message = message.astype(jnp.bfloat16)
    summed = jnp.sum(message.astype(jnp.float32).reshape(node_count, fanin, width), axis=1).astype(
        jnp.bfloat16
    )
    node_pre = jnp.dot(own_rows, node_in[0], preferred_element_type=jnp.float32)
    node_pre = (
        node_pre + jnp.dot(summed, node_in[1], preferred_element_type=jnp.float32) + biases[2]
    )
    node_hidden = jnp.maximum(node_pre, 0.0).astype(jnp.bfloat16)
    update = (
        layer_norm_rows(
            jnp.dot(node_hidden, node_out, preferred_element_type=jnp.float32) + biases[3]
        )
        * gains[1]
    )
    return (own_rows.astype(jnp.float32) + update).astype(jnp.bfloat16)


def project(rows_in, weight):
    return jnp.dot(rows_in, weight, preferred_element_type=jnp.float32).astype(jnp.bfloat16)


def join_rim(extended_rows, own_rows, rim_rows):
    return jnp.concatenate(
        [extended_rows[:rim_rows], own_rows, extended_rows[3 * rim_rows :]], axis=0
    )


def body(
    node_lat,
    edge_lat,
    edge_send,
    halo_list,
    pool_id,
    coarse_lat,
    cedge_lat,
    cedge_send,
    chalo_list,
    fine_edge_in,
    fine_edge_out,
    fine_node_in,
    fine_node_out,
    fine_bias,
    fine_gain,
    coarse_edge_in,
    coarse_edge_out,
    coarse_node_in,
    coarse_node_out,
    coarse_bias,
    coarse_gain,
):
    rim_rows = halo_list.shape[0] // 2
    extended_rows = padded(node_lat[halo_list], (("dom", 0),), rim_rows)
    sender_proj = project(join_rim(extended_rows, node_lat, rim_rows), fine_edge_in[0])
    fine_out = edge_node(
        sender_proj,
        node_lat,
        edge_lat,
        edge_send,
        fine_edge_in,
        fine_edge_out,
        fine_node_in,
        fine_node_out,
        fine_bias,
        fine_gain,
    )
    groups = lax.axis_size("group")
    cluster_rows = coarse_lat.shape[0]
    width = coarse_lat.shape[1]
    columns = groups * cluster_rows
    member_table = (pool_id[:, None] == jnp.arange(columns, dtype=jnp.int32)[None, :]).astype(
        jnp.bfloat16
    )
    cluster_sum = jnp.einsum(
        "nc,nh->ch", member_table, fine_out, preferred_element_type=jnp.float32
    )
    member_count = jnp.sum(member_table, axis=0, dtype=jnp.float32)
    got_sums, got_counts = (
        lax.all_to_all(
            cluster_sum.astype(jnp.bfloat16), "group", split_axis=0, concat_axis=0, tiled=True
        ).astype(cluster_sum.dtype),
        lax.all_to_all(
            member_count.astype(jnp.bfloat16), "group", split_axis=0, concat_axis=0, tiled=True
        ).astype(member_count.dtype),
    )
    cluster_sum = got_sums.reshape(groups, cluster_rows, width).sum(axis=0)
    member_count = got_counts.reshape(groups, cluster_rows).sum(axis=0)
    pooled_mean = cluster_sum / jnp.maximum(member_count, 1.0)[:, None]
    coarse_in = (coarse_lat.astype(jnp.float32) + pooled_mean).astype(jnp.bfloat16)
    coarse_rim = chalo_list.shape[0] // 2
    coarse_ext = padded(coarse_in[chalo_list], (("dom", 0),), coarse_rim)
    coarse_sender = project(join_rim(coarse_ext, coarse_in, coarse_rim), coarse_edge_in[0])
    coarse_out = edge_node(
        coarse_sender,
        coarse_in,
        cedge_lat,
        cedge_send,
        coarse_edge_in,
        coarse_edge_out,
        coarse_node_in,
        coarse_node_out,
        coarse_bias,
        coarse_gain,
    )
    return (fine_out, coarse_out)


def solution(mesh):
    placed = (
        P(("group", "dom"), None),
        P(("group", "dom"), None),
        P(("group", "dom")),
        P(("group", "dom")),
        P(("group", "dom")),
        P(("group", "dom"), None),
        P(("group", "dom"), None),
        P(("group", "dom")),
        P(("group", "dom")),
        P(),
        P(),
        P(),
        P(),
        P(),
        P(),
        P(),
        P(),
        P(),
        P(),
        P(),
        P(),
    )
    return jax.shard_map(
        body,
        mesh=mesh,
        in_specs=placed,
        out_specs=(P(("group", "dom"), None), P(("group", "dom"), None)),
        check_vma=False,
    )
```

profile of v0, /device:TPU:1, one launch (start us, length us, event | category | flops | bytes accessed | tf_op | source)
XLA Modules:
  0.0 167.5 jit_solution(8862112744358992017)
XLA Ops:
  1.5 4.9 %gather_fusion = bf16[1024,256]{1,0:T(8,128)(2,1)S(1)} fusion(bf16[2048,256]{1,0:T(8,128)(2,1)} %param.21, s32[1024]{0:T(1024)S(1)} %fusion.72), kind=kCustom, calls=%fused_computation | custom fusion | bytes 1052672 | tf_op jit(solution)/shard_map/gather | solution.py:100
  6.5 4.6 %collective-permute-start = (bf16[512,256]{1,0:T(8,128)(2,1)S(1)}, bf16[512,256]{1,0:T(8,128)(2,1)S(1)}, u32[]{:S(2)}, u32[]{:S(2)}) collective-permute-start(bf16[512,256]{1,0:T(8,128)(2,1)S(1)} %get-tuple-element.10), channel_id=1, source_target_pairs={{0,1},{1,2},{2,3},{3,4},{4,5},{5,6},{6,7},{8,9},{9,10},{10,11},{11... | collective-permute-start | bytes 786440 | tf_op jit(solution)/shard_map/ppermute | solution.py:14
  11.1 1.9 %collective-permute-start.1 = (bf16[512,256]{1,0:T(8,128)(2,1)S(1)}, bf16[512,256]{1,0:T(8,128)(2,1)}, u32[]{:S(2)}, u32[]{:S(2)}) collective-permute-start(bf16[512,256]{1,0:T(8,128)(2,1)S(1)} %get-tuple-element.11), channel_id=1, source_target_pairs={{1,0},{2,1},{3,2},{4,3},{5,4},{6,5},{7,6},{9,8},{10,9},{11,10},{12... | collective-permute-start | bytes 786440 | tf_op jit(solution)/shard_map/ppermute | solution.py:17
  15.8 3.4 %all-to-all-start.1 = ((bf16[4,2,128]{2,1,0:T(2,128)(2,1)}), bf16[4,2,128]{2,1,0:T(2,128)(2,1)S(1)}, u32[]{:S(2)}, u32[]{:S(2)}) async-start(bf16[4,2,128]{2,1,0:T(2,128)(2,1)} %reshape.124), calls=%async_computation.1 | async-start | bytes 4096 | tf_op jit(solution)/shard_map/all_to_all | solution.py:129
  19.8 2.7 %fusion.48 = f32[2048,256]{1,0:T(8,128)} fusion(bf16[2048,256]{1,0:T(8,128)(2,1)S(1)} %copy-done.2, bf16[3,256,256]{2,1,0:T(8,128)(2,1)} %param.30), kind=kOutput, calls=%fused_computation.67 | convolution fusion | flops 268435456 | bytes 3276800 | tf_op jit(solution)/shard_map/dot_general | solution.py:35
  23.1 1.7 %fusion.53 = f32[2048,256]{1,0:T(8,128)} fusion(bf16[2048,256]{1,0:T(8,128)(2,1)S(1)} %copy-done.2, bf16[2,256,256]{2,1,0:T(8,128)(2,1)S(1)} %copy-done.4), kind=kOutput, calls=%fused_computation.71 | convolution fusion | flops 268435456 | bytes 3276800 | tf_op jit(solution)/shard_map/dot_general | solution.py:52
  28.0 5.7 %add.199 = f32[2048,4,256]{2,1,0:T(4,128)} broadcast(f32[2048,256]{1,0:T(8,128)} %fusion.48), dimensions={0,2} | broadcast | bytes 10485760 | tf_op jit(solution)/shard_map/add | solution.py:38
  33.8 10.0 %add.200 = f32[8192,256]{1,0:T(8,128)} reshape(f32[2048,4,256]{2,1,0:T(4,128)} %add.199) | data formatting | bytes 16777216 | tf_op jit(solution)/shard_map/add | solution.py:38
  46.9 35.9 %gather_fusion.1 = bf16[8192,256]{1,0:T(8,128)(2,1)} fusion(bf16[3072,256]{1,0:T(8,128)(2,1)S(1)} %convolution_convert_fusion, s32[8192]{0:T(1024)} %fusion.71), kind=kCustom, calls=%fused_computation.1 | custom fusion | bytes 8421376 | tf_op jit(solution)/shard_map/gather | solution.py:37
  82.8 11.6 %fusion.86 = (f32[8192]{0:T(1024)S(1)}, f32[8192,256]{1,0:T(8,128)}) fusion(f32[256]{0:T(256)S(1)} %bitcast.79, bf16[256,256]{1,0:T(8,128)(2,1)S(1)} %copy-done.8, f32[8192,256]{1,0:T(8,128)} %add.200, bf16[8192,256]{1,0:T(8,128)(2,1)} %param.22, bf16[8192,256]{1,0:T(8,128)(2,1)} %gather_fusion.1, f32[256]{0:T(256)S(1)} %bitcast.80, ...), kind=kOutput, calls=%fused_computation.115 | convolution fusion | flops 2164252672 | bytes 25462784 | tf_op jit(solution)/shard_map/dot_general | solution.py:44
  94.5 5.4 %multiply_reduce_fusion = f32[8192]{0:T(1024)S(1)} fusion(f32[8192,256]{1,0:T(8,128)} %get-tuple-element.27, f32[8192]{0:T(1024)S(1)} %broadcast_multiply_fusion), kind=kLoop, calls=%fused_computation.12 | loop fusion | flops 6283264 | bytes 8454144 | tf_op jit(solution)/shard_map/reduce_sum | solution.py:25
  100.3 5.4 %multiply_convert_fusion = bf16[8192,256]{1,0:T(8,128)(2,1)} fusion(f32[8192,256]{1,0:T(8,128)S(1)} %copy-done.1, f32[256]{0:T(256)S(1)} %bitcast.74, f32[8192]{0:T(1024)S(1)} %add_rsqrt_fusion, f32[8192]{0:T(1024)S(1)} %broadcast_multiply_fusion), kind=kLoop, calls=%fused_computation.11 | loop fusion | flops 8388608 | bytes 12649472 | tf_op jit(solution)/shard_map/convert_element_type | solution.py:48
  105.7 6.9 %reshape.84 = bf16[2048,4,256]{2,1,0:T(4,128)(2,1)} reshape(bf16[8192,256]{1,0:T(8,128)(2,1)} %multiply_convert_fusion) | data formatting | bytes 8388608 | tf_op jit(solution)/shard_map/reshape | solution.py:49
  112.6 12.3 %reduce.2 = bf16[2048,256]{1,0:T(8,128)(2,1)} reduce(bf16[2048,4,256]{2,1,0:T(4,128)(2,1)} %reshape.84, bf16[]{:T(256)} %constant.16.clone.1), dimensions={1}, to_apply=%region_2.0.clone | reduce | flops 1572864 | bytes 5242882 | tf_op jit(solution)/shard_map/reduce_sum | solution.py:49
  124.9 2.8 %fusion.89 = (f32[2048]{0:T(1024)S(1)}, f32[2048,256]{0,1:T(8,128)S(1)}) fusion(f32[256]{0:T(256)S(1)} %bitcast.78, bf16[256,256]{1,0:T(8,128)(2,1)S(1)} %copy-done.9, f32[2048,256]{1,0:T(8,128)} %fusion.53, bf16[2048,256]{1,0:T(8,128)(2,1)} %reduce.2, f32[256]{0:T(256)S(1)} %bitcast.77, bf16[2,256,256]{2,1,0:T(8,128)(2,1)S(1)} %copy-done.4), kind=kOutput, calls=%fused_computation.116 | convolution fusion | flops 540014592 | bytes 5515264 | tf_op jit(solution)/shard_map/dot_general | solution.py:59
  128.0 1.7 %add_convert_fusion = bf16[2048,256]{0,1:T(8,128)(2,1)S(1)} fusion(bf16[2048,256]{0,1:T(8,128)(2,1)} %copy.46, f32[2048,256]{0,1:T(8,128)S(1)} %get-tuple-element.29, f32[256]{0:T(256)S(1)} %bitcast.73, f32[2048]{0:T(1024)S(1)} %add_rsqrt_fusion.1, f32[2048]{0:T(1024)S(1)} %broadcast_multiply_fusion.1), kind=kLoop, calls=%fused_computation.23 | loop fusion | flops 3145728 | bytes 4211712 | tf_op jit(solution)/shard_map/convert_element_type | solution.py:63
  130.7 2.5 %fusion.21 = bf16[1024,256]{1,0:T(8,128)(2,1)} fusion(bf16[2048,256]{0,1:T(8,128)(2,1)S(1)} %add_convert_fusion, s32[2048]{0:T(1024)S(1)} %copy-done.29), kind=kOutput, calls=%fused_computation.36 | convolution fusion | flops 1078198272 | bytes 1581056 | tf_op jit(solution)/shard_map/nc,nh->ch/dot_general | solution.py:121
  133.2 3.8 %all-to-all-start = ((bf16[4,256,256]{2,1,0:T(8,128)(2,1)}), bf16[4,256,256]{2,1,0:T(8,128)(2,1)S(1)}, u32[]{:S(2)}, u32[]{:S(2)}) async-start(bf16[4,256,256]{2,1,0:T(8,128)(2,1)} %bitcast.11), calls=%async_computation | async-start | bytes 1048576 | tf_op jit(solution)/shard_map/all_to_all | solution.py:126
  137.0 2.3 %copy.53 = bf16[2048,256]{1,0:T(8,128)(2,1)} copy(bf16[2048,256]{0,1:T(8,128)(2,1)} %copy-done.3) | data formatting | bytes 2097152
  139.2 5.3 %all-to-all-done = bf16[4,256,256]{2,1,0:T(8,128)(2,1)S(1)} async-done(((bf16[4,256,256]{2,1,0:T(8,128)(2,1)}), bf16[4,256,256]{2,1,0:T(8,128)(2,1)S(1)}, u32[]{:S(2)}, u32[]{:S(2)}) %all-to-all-start) | async-done | bytes 524320 | tf_op jit(solution)/shard_map/all_to_all | solution.py:126
  146.2 4.4 %collective-permute-start.2 = (bf16[128,256]{0,1:T(8,128)(2,1)S(1)}, bf16[128,256]{0,1:T(8,128)(2,1)}, u32[]{:S(2)}, u32[]{:S(2)}) collective-permute-start(bf16[128,256]{0,1:T(8,128)(2,1)S(1)} %copy.55), channel_id=1, source_target_pairs={{0,1},{1,2},{2,3},{3,4},{4,5},{5,6},{6,7},{8,9},{9,10},{10,11},{11... | collective-permute-start | bytes 196616 | tf_op jit(solution)/shard_map/ppermute | solution.py:14
  150.7 1.9 %collective-permute-start.3 = (bf16[128,256]{0,1:T(8,128)(2,1)S(1)}, bf16[128,256]{0,1:T(8,128)(2,1)}, u32[]{:S(2)}, u32[]{:S(2)}) collective-permute-start(bf16[128,256]{0,1:T(8,128)(2,1)S(1)} %copy.56), channel_id=1, source_target_pairs={{1,0},{2,1},{3,2},{4,3},{5,4},{6,5},{7,6},{9,8},{10,9},{11,10},{12... | collective-permute-start | bytes 196616 | tf_op jit(solution)/shard_map/ppermute | solution.py:17
  153.7 2.7 %collective-permute-done.3 = bf16[128,256]{0,1:T(8,128)(2,1)} collective-permute-done((bf16[128,256]{0,1:T(8,128)(2,1)S(1)}, bf16[128,256]{0,1:T(8,128)(2,1)}, u32[]{:S(2)}, u32[]{:S(2)}) %collective-permute-start.3) | collective-permute-done | bytes 65568 | tf_op jit(solution)/shard_map/ppermute | solution.py:17
  157.6 3.9 %gather_fusion.3 = bf16[1024,256]{1,0:T(8,128)(2,1)S(1)} fusion(bf16[512,256]{1,0:T(8,128)(2,1)S(1)} %convolution_convert_fusion.1, s32[1024]{0:T(1024)S(1)} %fusion.73), kind=kCustom, calls=%fused_computation.3 | custom fusion | bytes 1052672 | tf_op jit(solution)/shard_map/gather | solution.py:37
  (116 shorter events, 22.5 us)
Async XLA Ops:
  0.6 160.9 %copy-start = (bf16[1024,256]{1,0:T(8,128)(2,1)S(1)}, bf16[1024,256]{1,0:T(8,128)(2,1)}, u32[]{:S(2)}) copy-start(bf16[1024,256]{1,0:T(8,128)(2,1)} %param.27) | copy-start | bytes 1572868
  0.6 19.2 %copy-start.2 = (bf16[2048,256]{1,0:T(8,128)(2,1)S(1)}, bf16[2048,256]{1,0:T(8,128)(2,1)}, u32[]{:S(2)}) copy-start(bf16[2048,256]{1,0:T(8,128)(2,1)} %param.21) | copy-start | bytes 3145732
  0.7 12.3 %copy-start.28 = (s32[2048]{0:T(1024)S(1)}, s32[2048]{0:T(1024)}, u32[]{:S(2)}) copy-start(s32[2048]{0:T(1024)} %param.25) | copy-start | bytes 24580
  0.7 18.5 %copy-start.21 = (f32[4,256]{1,0:T(4,128)S(1)}, f32[4,256]{1,0:T(4,128)}, u32[]{:S(2)}) copy-start(f32[4,256]{1,0:T(4,128)} %param.34) | copy-start | bytes 12292
  1.5 21.0 %copy-start.24 = (f32[2,256]{1,0:T(2,128)S(1)}, f32[2,256]{1,0:T(2,128)}, u32[]{:S(2)}) copy-start(f32[2,256]{1,0:T(2,128)} %param.35) | copy-start | bytes 6148
  1.5 21.6 %copy-start.4 = (bf16[2,256,256]{2,1,0:T(8,128)(2,1)S(1)}, bf16[2,256,256]{2,1,0:T(8,128)(2,1)}, u32[]{:S(2)}) copy-start(bf16[2,256,256]{2,1,0:T(8,128)(2,1)} %param.32) | copy-start | bytes 786436
  6.4 18.5 %copy-start.22 = (s32[1024]{0:T(1024)S(1)}, s32[1024]{0:T(1024)}, u32[]{:S(2)}) copy-start(s32[1024]{0:T(1024)} %param.28) | copy-start | bytes 12292
  6.4 18.5 %copy-start.23 = (f32[4,256]{1,0:T(4,128)S(1)}, f32[4,256]{1,0:T(4,128)}, u32[]{:S(2)}) copy-start(f32[4,256]{1,0:T(4,128)} %param.40) | copy-start | bytes 12292
  6.4 19.1 %copy-start.25 = (f32[2,256]{1,0:T(2,128)S(1)}, f32[2,256]{1,0:T(2,128)}, u32[]{:S(2)}) copy-start(f32[2,256]{1,0:T(2,128)} %param.41) | copy-start | bytes 6148
  6.4 19.6 %copy-start.26 = (s32[256]{0:T(256)S(1)}, s32[256]{0:T(256)}, u32[]{:S(2)}) copy-start(s32[256]{0:T(256)} %param.29) | copy-start | bytes 3076
  6.5 38.1 %collective-permute-start = (bf16[512,256]{1,0:T(8,128)(2,1)S(1)}, bf16[512,256]{1,0:T(8,128)(2,1)S(1)}, u32[]{:S(2)}, u32[]{:S(2)}) collective-permute-start(bf16[512,256]{1,0:T(8,128)(2,1)S(1)} %get-tuple-element.10), channel_id=1, source_target_pairs={{0,1},{1,2},{2,3},{3,4},{4,5},{5,6},{6,7},{8,9},{9,10},{10,11},{11... | collective-permute-start | bytes 786440 | tf_op jit(solution)/shard_map/ppermute | solution.py:14
  11.1 34.2 %collective-permute-start.1 = (bf16[512,256]{1,0:T(8,128)(2,1)S(1)}, bf16[512,256]{1,0:T(8,128)(2,1)}, u32[]{:S(2)}, u32[]{:S(2)}) collective-permute-start(bf16[512,256]{1,0:T(8,128)(2,1)S(1)} %get-tuple-element.11), channel_id=1, source_target_pairs={{1,0},{2,1},{3,2},{4,3},{5,4},{6,5},{7,6},{9,8},{10,9},{11,10},{12... | collective-permute-start | bytes 786440 | tf_op jit(solution)/shard_map/ppermute | solution.py:17
  15.8 117.4 %all-to-all-start.1 = ((bf16[4,2,128]{2,1,0:T(2,128)(2,1)}), bf16[4,2,128]{2,1,0:T(2,128)(2,1)S(1)}, u32[]{:S(2)}, u32[]{:S(2)}) async-start(bf16[4,2,128]{2,1,0:T(2,128)(2,1)} %reshape.124), calls=%async_computation.1 | async-start | bytes 4096 | tf_op jit(solution)/shard_map/all_to_all | solution.py:129
  46.9 35.9 %copy-start.8 = (bf16[256,256]{1,0:T(8,128)(2,1)S(1)}, bf16[256,256]{1,0:T(8,128)(2,1)}, u32[]{:S(2)}) copy-start(bf16[256,256]{1,0:T(8,128)(2,1)} %param.31) | copy-start | bytes 393220
  46.9 35.9 %copy-start.18 = (f32[1,256]{1,0:T(1,128)S(1)}, f32[1,256]{1,0:T(1,128)}, u32[]{:S(2)}) copy-start(f32[1,256]{1,0:T(1,128)} %get-tuple-element.19) | copy-start | bytes 3076
  46.9 35.9 %copy-start.19 = (f32[1,256]{1,0:T(1,128)S(1)}, f32[1,256]{1,0:T(1,128)}, u32[]{:S(2)}) copy-start(f32[1,256]{1,0:T(1,128)} %get-tuple-element.20) | copy-start | bytes 3076
  112.6 12.3 %copy-start.9 = (bf16[256,256]{1,0:T(8,128)(2,1)S(1)}, bf16[256,256]{1,0:T(8,128)(2,1)}, u32[]{:S(2)}) copy-start(bf16[256,256]{1,0:T(8,128)(2,1)} %param.33) | copy-start | bytes 393220
  112.6 12.3 %copy-start.16 = (f32[1,256]{1,0:T(1,128)S(1)}, f32[1,256]{1,0:T(1,128)}, u32[]{:S(2)}) copy-start(f32[1,256]{1,0:T(1,128)} %get-tuple-element.18) | copy-start | bytes 3076
  112.6 12.3 %copy-start.17 = (f32[1,256]{1,0:T(1,128)S(1)}, f32[1,256]{1,0:T(1,128)}, u32[]{:S(2)}) copy-start(f32[1,256]{1,0:T(1,128)} %get-tuple-element.21) | copy-start | bytes 3076
  133.1 19.5 %copy-start.7 = (bf16[3,256,256]{2,1,0:T(8,128)(2,1)S(1)}, bf16[3,256,256]{2,1,0:T(8,128)(2,1)}, u32[]{:S(2)}) copy-start(bf16[3,256,256]{2,1,0:T(8,128)(2,1)} %param.36) | copy-start | bytes 1179652
  133.1 19.8 %copy-start.5 = (bf16[2,256,256]{2,1,0:T(8,128)(2,1)S(1)}, bf16[2,256,256]{2,1,0:T(8,128)(2,1)}, u32[]{:S(2)}) copy-start(bf16[2,256,256]{2,1,0:T(8,128)(2,1)} %param.38) | copy-start | bytes 786436
  133.2 11.4 %all-to-all-start = ((bf16[4,256,256]{2,1,0:T(8,128)(2,1)}), bf16[4,256,256]{2,1,0:T(8,128)(2,1)S(1)}, u32[]{:S(2)}, u32[]{:S(2)}) async-start(bf16[4,256,256]{2,1,0:T(8,128)(2,1)} %bitcast.11), calls=%async_computation | async-start | bytes 1048576 | tf_op jit(solution)/shard_map/all_to_all | solution.py:126
  146.2 7.5 %collective-permute-start.2 = (bf16[128,256]{0,1:T(8,128)(2,1)S(1)}, bf16[128,256]{0,1:T(8,128)(2,1)}, u32[]{:S(2)}, u32[]{:S(2)}) collective-permute-start(bf16[128,256]{0,1:T(8,128)(2,1)S(1)} %copy.55), channel_id=1, source_target_pairs={{0,1},{1,2},{2,3},{3,4},{4,5},{5,6},{6,7},{8,9},{9,10},{10,11},{11... | collective-permute-start | bytes 196616 | tf_op jit(solution)/shard_map/ppermute | solution.py:14
  150.7 5.7 %collective-permute-start.3 = (bf16[128,256]{0,1:T(8,128)(2,1)S(1)}, bf16[128,256]{0,1:T(8,128)(2,1)}, u32[]{:S(2)}, u32[]{:S(2)}) collective-permute-start(bf16[128,256]{0,1:T(8,128)(2,1)S(1)} %copy.56), channel_id=1, source_target_pairs={{1,0},{2,1},{3,2},{4,3},{5,4},{6,5},{7,6},{9,8},{10,9},{11,10},{12... | collective-permute-start | bytes 196616 | tf_op jit(solution)/shard_map/ppermute | solution.py:17
  (12 other events, 63.7 us)
where the time goes:
time: 169 us; the launch traced here: 167 us
  local copies, waits for them, and re-layouts  79.9 us (47%)
  other arithmetic  31.1 us (18%)
  matrix products  27.2 us (16%)
  starting transfers between devices  20.1 us (12%)
  waiting for transfers between devices  8 us (5%)
    gather x2, local copies, waits for them, and re-layouts, edge_node(): edge_pre = edge_pre + sender_proj[senders].astype(jnp.float32) + biases[0]  39.8 us
    add x4, local copies, waits for them, and re-layouts, edge_node(): edge_pre.reshape(node_count, fanin, width) + receiver_proj[:, None, :]  16.3 us
    dot_general x2, matrix products, edge_node(): jnp.dot(edge_hidden, edge_out, preferred_element_type=jnp.float32)  13.2 us
    reduce_sum x2, other arithmetic, edge_node(): jnp.sum(message.astype(jnp.float32).reshape(node_count, fanin, width), ax...  13 us
    ppermute x2, starting transfers between devices, padded(): lax.ppermute(lax.slice_in_dim(block, block.shape[dim] - width, None, axis...  9.03 us
    unnamed x69, local copies, waits for them, and re-layouts  8.11 us
    reshape x2, local copies, waits for them, and re-layouts, edge_node(): message.astype(jnp.float32).reshape(node_count, fanin, width)  7.02 us
    convert_element_type x2, other arithmetic, edge_node(): message = message.astype(jnp.bfloat16)  6.36 us
  transfers between devices with their start and end apart: 6, of which 2 were waited for; matrix products, arithmetic and copies ran while one was open for 70% of the time, Pallas kernels for 0%

commit v1 on v0

v1 whole, which is shorter than its diff:
```python
import functools

import jax
import jax.numpy as jnp
from jax import lax
from jax.experimental import pallas as pl
from jax.experimental.pallas import tpu as pltpu
from jax.sharding import PartitionSpec as P

EPSILON = 1e-05
F32 = jnp.float32
BF16 = jnp.bfloat16
NT = 128
DEG = 4


def dot(a, b):
    return jnp.dot(a, b, preferred_element_type=F32)


def centre(weight):
    w = weight.astype(F32)
    return (w - jnp.mean(w, axis=-1, keepdims=True)).astype(BF16)


def unit_rows(z):
    return z * lax.rsqrt(jnp.mean(z * z, axis=-1, keepdims=True) + EPSILON)


def fine_kernel(
    groups, clusters,
    send, pool, node, low, high, edge, ein, eout, nin, nout, bias, gain,
    out, part,
    table, proj, scale, gath, pre_lo, pre_hi, recv, npre, eoc, noc, bc, acc, cnt,
):
    step = pl.program_id(0)
    steps = pl.num_programs(0)
    rows = node.shape[0]
    rim = low.shape[0]
    et = NT * DEG

    def fetch(tile, k, n):
        at = send[tile * et + n * DEG + k]
        gath[pl.ds(k * NT + n, 1), :] = table[pl.ds(at, 1), :]

    @pl.when(step == 0)
    def _():
        eoc[...] = centre(eout[...])
        noc[...] = centre(nout[...])
        b = bias[...]
        bc[...] = b - jnp.mean(b, axis=-1, keepdims=True)
        top = jnp.zeros((1, 256), F32)
        for ref, start in ((low, 0), (node, rim), (high, rim + rows)):
            for r in range(0, ref.shape[0], 256):
                p = dot(ref[r:r + 256, :], ein[0])
                proj[start + r:start + r + 256, :] = p
                top = jnp.maximum(top, jnp.max(jnp.abs(p), axis=0, keepdims=True))
        top = jnp.maximum(top, 1e-20)
        scale[...] = top * (1.0 / 32767.0)
        inv = 32767.0 / top
        for r in range(0, rows + 2 * rim, 256):
            q = jnp.round(proj[r:r + 256, :] * inv).astype(jnp.int32)
            table[r:r + 256, :] = (q[:, :128] & 0xFFFF) | (q[:, 128:] << 16)
        for r in range(0, rows, 256):
            own = node[r:r + 256, :]
            recv[r:r + 256, :] = dot(own, ein[1]) + bias[0:1, :]
            npre[r:r + 256, :] = dot(own, nin[0]) + bias[2:3, :]
        acc[...] = jnp.zeros_like(acc)
        cnt[...] = jnp.zeros_like(cnt)

        def first(n, carry):
            for k in range(DEG):
                fetch(0, k, n)
            return carry

        lax.fori_loop(0, NT, first, 0, unroll=8)

    base = pl.multiple_of(step * NT, NT)
    nxt = jnp.minimum(step + 1, steps - 1)
    p = dot(edge[...], ein[2])
    pre_lo[...] = p[:, :128]
    pre_hi[...] = p[:, 128:]
    rv = recv[pl.ds(base, NT), :]
    total = jnp.zeros((NT, 256), F32)
    for k in range(DEG):
        g = gath[k * NT:(k + 1) * NT, :]
        s = jnp.concatenate([(g << 16) >> 16, g >> 16], axis=1).astype(F32) * scale[...]
        e = jnp.concatenate(
            [pre_lo[pl.ds(k, NT, stride=DEG), :], pre_hi[pl.ds(k, NT, stride=DEG), :]], axis=1
        )
        h = jnp.maximum(e + s + rv, 0.0).astype(BF16)
        total = total + unit_rows(dot(h, eoc[...]) + bc[1:2, :])
        for n in range(NT):
            fetch(nxt, k, n)
    summed = (total * gain[0:1, :]).astype(BF16)
    h = jnp.maximum(npre[pl.ds(base, NT), :] + dot(summed, nin[1]), 0.0).astype(BF16)
    update = unit_rows(dot(h, noc[...]) + bc[3:4, :]) * gain[1:2, :]
    result = (node[pl.ds(base, NT), :].astype(F32) + update).astype(BF16)
    out[...] = result
    ids = pool[pl.ds(step, 1), :]
    ones = jnp.ones((16, NT), BF16)
    for g in range(groups):
        c = g * clusters
        names = lax.broadcasted_iota(jnp.int32, (clusters, NT), 0) + c
        member = jnp.where(names == ids, 1.0, 0.0).astype(BF16)
        acc[c:c + clusters, :] += dot(member, result)
        cnt[g] += lax.dot_general(
            ones, member, (((1,), (1,)), ((), ())), preferred_element_type=F32
        )

    @pl.when(step == steps - 1)
    def _():
        for g in range(groups):
            c = g * clusters
            part[g, 0:clusters, :] = acc[c:c + clusters, :].astype(BF16)
            n = cnt[g]
            big = jnp.floor(n * (1.0 / 256.0)) * 256.0
            which = lax.broadcasted_iota(jnp.int32, n.shape, 0)
            part[g, clusters:clusters + 16, :] = jnp.where(
                which == 0, n - big, jnp.where(which == 1, big, 0.0)
            ).astype(BF16)


def fine_level(groups, clusters, send, pool, node, low, high, edge, ein, eout, nin, nout, bias, gain):
    rows, width = node.shape
    rim = low.shape[0]
    steps = rows // NT
    et = NT * DEG
    whole = pl.BlockSpec(memory_space=pltpu.VMEM)
    return pl.pallas_call(
        functools.partial(fine_kernel, groups, clusters),
        grid=(steps,),
        in_specs=[pl.BlockSpec(memory_space=pltpu.SMEM), whole, whole, whole, whole,
                  pl.BlockSpec((et, width), lambda i: (i, 0))] + [whole] * 6,
        out_specs=[pl.BlockSpec((NT, width), lambda i: (i, 0)),
                   pl.BlockSpec((groups, clusters + 16, width), lambda i: (0, 0, 0))],
        out_shape=[jax.ShapeDtypeStruct((rows, width), BF16),
                   jax.ShapeDtypeStruct((groups, clusters + 16, width), BF16)],
        scratch_shapes=[
            pltpu.VMEM((rows + 2 * rim, 128), jnp.int32),
            pltpu.VMEM((rows + 2 * rim, width), F32),
            pltpu.VMEM((1, width), F32),
            pltpu.VMEM((et, 128), jnp.int32),
            pltpu.VMEM((et, 128), F32),
            pltpu.VMEM((et, 128), F32),
            pltpu.VMEM((rows, width), F32),
            pltpu.VMEM((rows, width), F32),
            pltpu.VMEM((width, width), BF16),
            pltpu.VMEM((width, width), BF16),
            pltpu.VMEM((4, width), F32),
            pltpu.VMEM((groups * clusters, width), F32),
            pltpu.VMEM((groups, 16, clusters), F32),
        ],
        compiler_params=pltpu.CompilerParams(vmem_limit_bytes=48 * 1024 * 1024),
        cost_estimate=pl.CostEstimate(flops=7_000_000_000, bytes_accessed=9_000_000, transcendentals=0),
        name="fine_level",
    )(send, pool.reshape(steps, NT), node, low, high, edge, ein, eout, nin, nout, bias, gain)


def border(rows, chosen):
    table = (chosen[:, None] == jnp.arange(rows.shape[0], dtype=jnp.int32)[None, :]).astype(BF16)
    return dot(table, rows).astype(BF16)


def exchange(edge_rows, rim):
    count = lax.axis_size("dom")
    forward = [(i, i + 1) for i in range(count - 1)]
    backward = [(t, s) for s, t in forward]
    return (lax.ppermute(edge_rows[rim:], "dom", forward),
            lax.ppermute(edge_rows[:rim], "dom", backward))


def layer_norm_rows(values):
    row_mean = jnp.mean(values, axis=-1, keepdims=True)
    centred = values - row_mean
    variance = jnp.mean(centred * centred, axis=-1, keepdims=True)
    return centred * lax.rsqrt(variance + EPSILON)


def edge_node(
    sender_proj, own_rows, edge_rows, senders, edge_in, edge_out, node_in, node_out, biases, gains
):
    node_count = own_rows.shape[0]
    width = own_rows.shape[1]
    fanin = edge_rows.shape[0] // node_count
    receiver_proj = dot(own_rows, edge_in[1])
    edge_pre = dot(edge_rows, edge_in[2])
    edge_pre = edge_pre + sender_proj[senders].astype(F32) + biases[0]
    edge_pre = (edge_pre.reshape(node_count, fanin, width) + receiver_proj[:, None, :]).reshape(
        node_count * fanin, width
    )
    edge_hidden = jnp.maximum(edge_pre, 0.0).astype(BF16)
    message = layer_norm_rows(dot(edge_hidden, edge_out) + biases[1]) * gains[0]
    message = message.astype(BF16)
    summed = jnp.sum(message.astype(F32).reshape(node_count, fanin, width), axis=1).astype(BF16)
    node_pre = dot(own_rows, node_in[0]) + dot(summed, node_in[1]) + biases[2]
    node_hidden = jnp.maximum(node_pre, 0.0).astype(BF16)
    update = layer_norm_rows(dot(node_hidden, node_out) + biases[3]) * gains[1]
    return (own_rows.astype(F32) + update).astype(BF16)


def body(
    node_lat, edge_lat, edge_send, halo_list, pool_id,
    coarse_lat, cedge_lat, cedge_send, chalo_list,
    fine_edge_in, fine_edge_out, fine_node_in, fine_node_out, fine_bias, fine_gain,
    coarse_edge_in, coarse_edge_out, coarse_node_in, coarse_node_out, coarse_bias, coarse_gain,
):
    groups = lax.axis_size("group")
    clusters, width = coarse_lat.shape
    rim = halo_list.shape[0] // 2
    low, high = exchange(border(node_lat, halo_list), rim)
    fine_out, part = fine_level(
        groups, clusters, edge_send, pool_id, node_lat, low, high, edge_lat,
        fine_edge_in, fine_edge_out, fine_node_in, fine_node_out, fine_bias, fine_gain,
    )
    got = lax.all_to_all(part, "group", split_axis=0, concat_axis=0, tiled=True).astype(F32)
    got = got.sum(axis=0)
    cluster_sum = got[:clusters]
    member_count = got[clusters] + got[clusters + 1]
    pooled_mean = cluster_sum / jnp.maximum(member_count, 1.0)[:, None]
    coarse_in = (coarse_lat.astype(F32) + pooled_mean).astype(BF16)
    crim = chalo_list.shape[0] // 2
    clow, chigh = exchange(border(coarse_in, chalo_list), crim)
    cext = jnp.concatenate([clow, coarse_in, chigh], axis=0)
    coarse_out = edge_node(
        dot(cext, coarse_edge_in[0]).astype(BF16),
        coarse_in, cedge_lat, cedge_send,
        coarse_edge_in, coarse_edge_out, coarse_node_in, coarse_node_out, coarse_bias, coarse_gain,
    )
    return (fine_out, coarse_out)


def solution(mesh):
    both = ("group", "dom")
    rows, flat = P(both, None), P(both)
    placed = (rows, rows, flat, flat, flat, rows, rows, flat, flat) + (P(),) * 12
    return jax.shard_map(body, mesh=mesh, in_specs=placed, out_specs=(rows, rows), check_vma=False)
```

time: 169 us -> 75.5 us (0.45)
  local copies, waits for them, and re-layouts: 79.9 us -> 8.74 us
  other arithmetic: 31.1 us -> 2.36 us
  Pallas kernels: 0 us -> 26.1 us
  matrix products: 27.2 us -> 8.51 us
  waiting for transfers between devices: 8 us -> 10.8 us
  starting transfers between devices: 20.1 us -> 17.6 us
    gather x4 -> x1, local copies, waits for them, and re-layouts: 45.8 us -> 3.94 us  [edge_node(): edge_pre = edge_pre + sender_proj[senders].astype(F32) + biases[0]]
    pallas_call x0 -> x1, Pallas kernels: none -> 26.1 us  [fine_level(): pl.pallas_call(functools.partial(fine_kernel, groups, clusters), grid=(st...]
    dot_general x11 -> x7, matrix products: 27.2 us -> 8.51 us  [dot(): return jnp.dot(a, b, preferred_element_type=F32)]
    add x4 -> x2, local copies, waits for them, and re-layouts: 16.3 us -> 0.54 us  [edge_node(): edge_pre.reshape(node_count, fanin, width) + receiver_proj[:, None, :]]
    reduce_sum x5 -> x2, other arithmetic: 14.1 us -> 0.75 us  [the longest x1 0.67 us: edge_node(): jnp.sum(message.astype(F32).reshape(node_count, fanin, width), axis=1)]
    convert_element_type x5 -> x3, other arithmetic: 8.23 us -> 1.16 us  [the longest x1 1.01 us: edge_node(): message = message.astype(BF16)]
    reshape x2 -> x1, local copies, waits for them, and re-layouts: 7.02 us -> 0.12 us  [edge_node(): message.astype(F32).reshape(node_count, fanin, width)]
    unnamed x69 -> x35, local copies, waits for them, and re-layouts: 8.11 us -> 1.97 us
  transfers between devices with their start and end apart: 6 -> 5, of which waited for: 2 -> 4; matrix products, arithmetic and copies ran while one was open for 70% -> 6% of each run, Pallas kernels for 0% -> 0%
where the time goes in v1:
time: 75.5 us; the launch traced here: 75.2 us
  Pallas kernels  26.1 us (35%)
  starting transfers between devices  17.6 us (23%)
  waiting for transfers between devices  10.8 us (14%)
  local copies, waits for them, and re-layouts  8.74 us (12%)
  matrix products  8.51 us (11%)
  other arithmetic  2.36 us (3%)
  between operations  1.09 us (1%)
    pallas_call x1, Pallas kernels, fine_level(): pl.pallas_call(functools.partial(fine_kernel, groups, clusters), grid=(st...  26.1 us
    ppermute x2, starting transfers between devices, exchange(): lax.ppermute(edge_rows[rim:], 'dom', forward)  10.2 us
    dot_general x7, matrix products, dot(): return jnp.dot(a, b, preferred_element_type=F32)  8.51 us
    ppermute x2, waiting for transfers between devices, exchange(): lax.ppermute(edge_rows[:rim], 'dom', backward)  5.68 us
    all_to_all x1, waiting for transfers between devices, body(): lax.all_to_all(part, 'group', split_axis=0, concat_axis=0, tiled=True)  4.44 us
    gather x1, local copies, waits for them, and re-layouts, edge_node(): edge_pre = edge_pre + sender_proj[senders].astype(F32) + biases[0]  3.94 us
    ppermute x2, starting transfers between devices, exchange(): lax.ppermute(edge_rows[:rim], 'dom', backward)  3.84 us
    all_to_all x1, starting transfers between devices, body(): lax.all_to_all(part, 'group', split_axis=0, concat_axis=0, tiled=True)  3.61 us
  transfers between devices with their start and end apart: 5, of which 4 were waited for; matrix products, arithmetic and copies ran while one was open for 6% of the time, Pallas kernels for 0%

profile of v1, /device:TPU:1, one launch (start us, length us, event | category | flops | bytes accessed | tf_op | source)
XLA Modules:
  0.0 75.2 jit_solution(16629945853165245618)
XLA Ops:
  0.7 2.9 %fusion.6 = bf16[1024,256]{1,0:T(8,128)(2,1)S(1)} fusion(bf16[2048,256]{1,0:T(8,128)(2,1)} %node.1, s32[1024]{0:T(1024)} %param.24), kind=kOutput, calls=%fused_computation.10 | convolution fusion | flops 1076101120 | bytes 1576960 | tf_op jit(solution)/shard_map/dot_general | solution.py:18
  3.6 0.7 fusion.42
  4.4 4.6 %collective-permute-start = (bf16[512,256]{1,0:T(8,128)(2,1)}, bf16[512,256]{1,0:T(8,128)(2,1)S(1)}, u32[]{:S(2)}, u32[]{:S(2)}) collective-permute-start(bf16[512,256]{1,0:T(8,128)(2,1)} %get-tuple-element.13), channel_id=1, source_target_pairs={{0,1},{1,2},{2,3},{3,4},{4,5},{5,6},{6,7},{8,9},{9,10},{10,11},{11... | collective-permute-start | bytes 786440 | tf_op jit(solution)/shard_map/ppermute | solution.py:169
  8.9 1.9 %collective-permute-start.1 = (bf16[512,256]{1,0:T(8,128)(2,1)S(1)}, bf16[512,256]{1,0:T(8,128)(2,1)S(1)}, u32[]{:S(2)}, u32[]{:S(2)}) collective-permute-start(bf16[512,256]{1,0:T(8,128)(2,1)S(1)} %get-tuple-element.12), channel_id=1, source_target_pairs={{1,0},{2,1},{3,2},{4,3},{5,4},{6,5},{7,6},{9,8},{10,9},{11,10},{12... | collective-permute-start | bytes 786440 | tf_op jit(solution)/shard_map/ppermute | solution.py:170
  10.9 1.0 %copy.31 = bf16[256,256]{0,1:T(8,128)(2,1)S(1)} copy(bf16[256,256]{1,0:T(8,128)(2,1)} %param.26) | data formatting | bytes 262144 | tf_op args[5]
  11.9 0.6 collective-permute-done.low
  12.6 4.1 %collective-permute-done.1.high = bf16[512,256]{1,0:T(8,128)(2,1)S(1)} collective-permute-done((bf16[512,256]{1,0:T(8,128)(2,1)S(1)}, bf16[512,256]{1,0:T(8,128)(2,1)S(1)}, u32[]{:S(2)}, u32[]{:S(2)}) %collective-permute-start.1) | collective-permute-done | bytes 262176 | tf_op jit(solution)/shard_map/ppermute | solution.py:170
  16.7 26.1 %fine_level.1 = (bf16[2048,256]{1,0:T(8,128)(2,1)}, bf16[4,272,256]{2,1,0:T(8,128)(2,1)}) custom-call(s32[8192]{0:T(1024)S(1)} %copy-done.6, s32[16,128]{1,0:T(8,128)S(1)} %bitcast.37, bf16[2048,256]{1,0:T(8,128)(2,1)S(1)} %copy-done.1, bf16[512,256]{1,0:T(8,128)(2,1)S(1)} %collective-permute-done.low, bf16[512,256]{1,0:T(8,128)(2,1)S(1)} %collective-permute-done.1.high, ...), custom_call_target="tpu_custom_call" | custom-call | flops 7000000000 | bytes 9000000 | tf_op jit(solution)/shard_map/fine_level/pallas_call | solution.py:130
  42.8 3.6 %all-to-all-start = ((bf16[4,272,256]{2,1,0:T(8,128)(2,1)}), bf16[4,272,256]{2,1,0:T(8,128)(2,1)S(1)}, u32[]{:S(2)}, u32[]{:S(2)}) async-start(bf16[4,272,256]{2,1,0:T(8,128)(2,1)} %get-tuple-element.5), calls=%async_computation | async-start | bytes 1114112 | tf_op jit(solution)/shard_map/all_to_all | solution.py:216
  46.4 0.6 fusion.45
  47.0 0.6 fusion.44
  47.6 4.4 %all-to-all-done = bf16[4,272,256]{2,1,0:T(8,128)(2,1)S(1)} async-done(((bf16[4,272,256]{2,1,0:T(8,128)(2,1)}), bf16[4,272,256]{2,1,0:T(8,128)(2,1)S(1)}, u32[]{:S(2)}, u32[]{:S(2)}) %all-to-all-start) | async-done | bytes 557088 | tf_op jit(solution)/shard_map/all_to_all | solution.py:216
  52.6 5.6 %collective-permute-start.2 = (bf16[128,256]{1,0:T(8,128)(2,1)S(1)}, bf16[128,256]{1,0:T(8,128)(2,1)S(1)}, u32[]{:S(2)}, u32[]{:S(2)}) collective-permute-start(bf16[128,256]{1,0:T(8,128)(2,1)S(1)} %get-tuple-element.14), channel_id=1, source_target_pairs={{0,1},{1,2},{2,3},{3,4},{4,5},{5,6},{6,7},{8,9},{9,10},{10,11},{11... | collective-permute-start | bytes 196616 | tf_op jit(solution)/shard_map/ppermute | solution.py:169
  58.2 1.9 %collective-permute-start.3 = (bf16[128,256]{1,0:T(8,128)(2,1)S(1)}, bf16[128,256]{1,0:T(8,128)(2,1)S(1)}, u32[]{:S(2)}, u32[]{:S(2)}) collective-permute-start(bf16[128,256]{1,0:T(8,128)(2,1)S(1)} %get-tuple-element.15), channel_id=1, source_target_pairs={{1,0},{2,1},{3,2},{4,3},{5,4},{6,5},{7,6},{9,8},{10,9},{11,10},{12... | collective-permute-start | bytes 196616 | tf_op jit(solution)/shard_map/ppermute | solution.py:170
  60.1 1.1 %fusion.20 = f32[256,256]{1,0:T(8,128)S(1)} fusion(bf16[256,256]{0,1:T(8,128)(2,1)S(1)} %add_convert_fusion.1, bf16[3,256,256]{2,1,0:T(8,128)(2,1)} %param.36), kind=kOutput, calls=%fused_computation.34 | convolution fusion | flops 33554432 | bytes 524288 | tf_op jit(solution)/shard_map/dot_general | solution.py:18
  62.2 1.6 %collective-permute-done.3 = bf16[128,256]{1,0:T(8,128)(2,1)S(1)} collective-permute-done((bf16[128,256]{1,0:T(8,128)(2,1)S(1)}, bf16[128,256]{1,0:T(8,128)(2,1)S(1)}, u32[]{:S(2)}, u32[]{:S(2)}) %collective-permute-start.3) | collective-permute-done | bytes 65568 | tf_op jit(solution)/shard_map/ppermute | solution.py:170
  63.9 1.2 %convolution_convert_fusion = bf16[512,256]{1,0:T(8,128)(2,1)S(1)} fusion(bf16[128,256]{0,1:T(8,128)(2,1)S(1)} %copy.34, bf16[256,256]{0,1:T(8,128)(2,1)S(1)} %add_convert_fusion.1, bf16[128,256]{0,1:T(8,128)(2,1)S(1)} %copy.33, bf16[3,256,256]{2,1,0:T(8,128)(2,1)} %param.36), kind=kOutput, calls=%fused_computation.11 | convolution fusion | flops 68026368 | bytes 655360 | tf_op jit(solution)/shard_map/dot_general | solution.py:18
  65.1 3.9 %gather_fusion = bf16[1024,256]{1,0:T(8,128)(2,1)S(1)} fusion(bf16[512,256]{1,0:T(8,128)(2,1)S(1)} %convolution_convert_fusion, s32[1024]{0:T(1024)S(1)} %fusion.37), kind=kCustom, calls=%fused_computation | custom fusion | bytes 1052672 | tf_op jit(solution)/shard_map/gather | solution.py:188
  69.0 1.6 %fusion.46 = (f32[1024]{0:T(1024)S(1)}, f32[1024,256]{1,0:T(8,128)S(1)}) fusion(f32[256]{0:T(256)S(1)} %bitcast.40, bf16[256,256]{1,0:T(8,128)(2,1)} %param.37, f32[1024,256]{1,0:T(8,128)S(1)} %add.108, bf16[1024,256]{1,0:T(8,128)(2,1)S(1)} %copy-done, bf16[1024,256]{1,0:T(8,128)(2,1)S(1)} %gather_fusion, f32[256]{0:T(256)S(1)} %bitcast.41, ...), kind=kOutput, calls=%fused_computation.63 | convolution fusion | flops 270531584 | bytes 3414016 | tf_op jit(solution)/shard_map/dot_general | solution.py:18
  70.7 0.4 multiply_reduce_fusion
  71.0 1.0 %multiply_convert_fusion = bf16[1024,256]{1,0:T(8,128)(2,1)S(1)} fusion(f32[1024,256]{1,0:T(8,128)S(1)} %get-tuple-element.23, f32[256]{0:T(256)} %bitcast.42, f32[1024]{0:T(1024)S(1)} %add_rsqrt_fusion, f32[1024]{0:T(1024)S(1)} %broadcast_multiply_fusion), kind=kLoop, calls=%fused_computation.19 | loop fusion | flops 1048576 | bytes 1582080 | tf_op jit(solution)/shard_map/convert_element_type | solution.py:194
  72.2 0.7 reduce
  72.9 1.3 %fusion.49 = (f32[256]{0:T(256)S(1)}, f32[256,256]{0,1:T(8,128)S(1)}) fusion(f32[256]{0:T(256)} %bitcast.44, bf16[256,256]{1,0:T(8,128)(2,1)} %param.39, f32[256,256]{1,0:T(8,128)S(1)} %fusion.25, bf16[256,256]{1,0:T(8,128)(2,1)S(1)} %reduce, f32[256]{0:T(256)} %bitcast.43, bf16[2,256,256]{2,1,0:T(8,128)(2,1)S(1)} %copy-done.11), kind=kOutput, calls=%fused_computation.64 | convolution fusion | flops 67501824 | bytes 920576 | tf_op jit(solution)/shard_map/dot_general | solution.py:18
  74.4 0.8 %copy.35 = bf16[256,256]{1,0:T(8,128)(2,1)} copy(bf16[256,256]{0,1:T(8,128)(2,1)S(1)} %add_convert_fusion) | data formatting | bytes 262144
  (53 shorter events, 1.9 us)
Async XLA Ops:
  0.6 68.4 %copy-start = (bf16[1024,256]{1,0:T(8,128)(2,1)S(1)}, bf16[1024,256]{1,0:T(8,128)(2,1)}, u32[]{:S(2)}) copy-start(bf16[1024,256]{1,0:T(8,128)(2,1)} %param.27) | copy-start | bytes 1572868
  0.6 16.0 %copy-start.1 = (bf16[2048,256]{1,0:T(8,128)(2,1)S(1)}, bf16[2048,256]{1,0:T(8,128)(2,1)}, u32[]{:S(2)}) copy-start(bf16[2048,256]{1,0:T(8,128)(2,1)} %node.1) | copy-start | bytes 3145732
  0.7 11.2 %copy-start.12 = (s32[1024]{0:T(1024)S(1)}, s32[1024]{0:T(1024)}, u32[]{:S(2)}) copy-start(s32[1024]{0:T(1024)} %param.28) | copy-start | bytes 12292
  0.7 16.0 %copy-start.7 = (s32[2048]{0:T(1024)S(1)}, s32[2048]{0:T(1024)}, u32[]{:S(2)}) copy-start(s32[2048]{0:T(1024)} %param.25) | copy-start | bytes 24580
  0.7 16.0 %copy-start.6 = (s32[8192]{0:T(1024)S(1)}, s32[8192]{0:T(1024)}, u32[]{:S(2)}) copy-start(s32[8192]{0:T(1024)} %send.1) | copy-start | bytes 98308
  0.7 16.0 %copy-start.2 = (bf16[3,256,256]{2,1,0:T(8,128)(2,1)S(1)}, bf16[3,256,256]{2,1,0:T(8,128)(2,1)}, u32[]{:S(2)}) copy-start(bf16[3,256,256]{2,1,0:T(8,128)(2,1)} %ein.1) | copy-start | bytes 1179652
  0.7 16.0 %copy-start.4 = (bf16[256,256]{1,0:T(8,128)(2,1)S(1)}, bf16[256,256]{1,0:T(8,128)(2,1)}, u32[]{:S(2)}) copy-start(bf16[256,256]{1,0:T(8,128)(2,1)} %eout.1) | copy-start | bytes 393220
  0.7 16.0 %copy-start.3 = (bf16[2,256,256]{2,1,0:T(8,128)(2,1)S(1)}, bf16[2,256,256]{2,1,0:T(8,128)(2,1)}, u32[]{:S(2)}) copy-start(bf16[2,256,256]{2,1,0:T(8,128)(2,1)} %nin.1) | copy-start | bytes 786436
  0.7 16.0 %copy-start.5 = (bf16[256,256]{1,0:T(8,128)(2,1)S(1)}, bf16[256,256]{1,0:T(8,128)(2,1)}, u32[]{:S(2)}) copy-start(bf16[256,256]{1,0:T(8,128)(2,1)} %nout.1) | copy-start | bytes 393220
  0.7 16.0 %copy-start.8 = (f32[4,256]{1,0:T(4,128)S(1)}, f32[4,256]{1,0:T(4,128)}, u32[]{:S(2)}) copy-start(f32[4,256]{1,0:T(4,128)} %bias.1) | copy-start | bytes 12292
  0.7 16.0 %copy-start.9 = (f32[2,256]{1,0:T(2,128)S(1)}, f32[2,256]{1,0:T(2,128)}, u32[]{:S(2)}) copy-start(f32[2,256]{1,0:T(2,128)} %gain.1) | copy-start | bytes 6148
  4.4 8.2 %collective-permute-start = (bf16[512,256]{1,0:T(8,128)(2,1)}, bf16[512,256]{1,0:T(8,128)(2,1)S(1)}, u32[]{:S(2)}, u32[]{:S(2)}) collective-permute-start(bf16[512,256]{1,0:T(8,128)(2,1)} %get-tuple-element.13), channel_id=1, source_target_pairs={{0,1},{1,2},{2,3},{3,4},{4,5},{5,6},{6,7},{8,9},{9,10},{10,11},{11... | collective-permute-start | bytes 786440 | tf_op jit(solution)/shard_map/ppermute | solution.py:169
  8.9 7.7 %collective-permute-start.1 = (bf16[512,256]{1,0:T(8,128)(2,1)S(1)}, bf16[512,256]{1,0:T(8,128)(2,1)S(1)}, u32[]{:S(2)}, u32[]{:S(2)}) collective-permute-start(bf16[512,256]{1,0:T(8,128)(2,1)S(1)} %get-tuple-element.12), channel_id=1, source_target_pairs={{1,0},{2,1},{3,2},{4,3},{5,4},{6,5},{7,6},{9,8},{10,9},{11,10},{12... | collective-permute-start | bytes 786440 | tf_op jit(solution)/shard_map/ppermute | solution.py:170
  16.7 29.7 %copy-start.14 = (f32[2,256]{1,0:T(2,128)S(1)}, f32[2,256]{1,0:T(2,128)}, u32[]{:S(2)}) copy-start(f32[2,256]{1,0:T(2,128)} %param.41) | copy-start | bytes 6148
  16.7 30.3 %copy-start.13 = (f32[4,256]{1,0:T(4,128)S(1)}, f32[4,256]{1,0:T(4,128)}, u32[]{:S(2)}) copy-start(f32[4,256]{1,0:T(4,128)} %param.40) | copy-start | bytes 12292
  16.7 35.6 %copy-start.15 = (s32[256]{0:T(256)S(1)}, s32[256]{0:T(256)}, u32[]{:S(2)}) copy-start(s32[256]{0:T(256)} %param.29) | copy-start | bytes 3076
  42.8 18.5 %copy-start.10 = (bf16[2,256,256]{2,1,0:T(8,128)(2,1)S(1)}, bf16[2,256,256]{2,1,0:T(8,128)(2,1)}, u32[]{:S(2)}) copy-start(bf16[2,256,256]{2,1,0:T(8,128)(2,1)} %param.38) | copy-start | bytes 786436
  42.8 9.2 %all-to-all-start = ((bf16[4,272,256]{2,1,0:T(8,128)(2,1)}), bf16[4,272,256]{2,1,0:T(8,128)(2,1)S(1)}, u32[]{:S(2)}, u32[]{:S(2)}) async-start(bf16[4,272,256]{2,1,0:T(8,128)(2,1)} %get-tuple-element.5), calls=%async_computation | async-start | bytes 1114112 | tf_op jit(solution)/shard_map/all_to_all | solution.py:216
  52.6 9.5 %collective-permute-start.2 = (bf16[128,256]{1,0:T(8,128)(2,1)S(1)}, bf16[128,256]{1,0:T(8,128)(2,1)S(1)}, u32[]{:S(2)}, u32[]{:S(2)}) collective-permute-start(bf16[128,256]{1,0:T(8,128)(2,1)S(1)} %get-tuple-element.14), channel_id=1, source_target_pairs={{0,1},{1,2},{2,3},{3,4},{4,5},{5,6},{6,7},{8,9},{9,10},{10,11},{11... | collective-permute-start | bytes 196616 | tf_op jit(solution)/shard_map/ppermute | solution.py:169
  58.2 5.6 %collective-permute-start.3 = (bf16[128,256]{1,0:T(8,128)(2,1)S(1)}, bf16[128,256]{1,0:T(8,128)(2,1)S(1)}, u32[]{:S(2)}, u32[]{:S(2)}) collective-permute-start(bf16[128,256]{1,0:T(8,128)(2,1)S(1)} %get-tuple-element.15), channel_id=1, source_target_pairs={{1,0},{2,1},{3,2},{4,3},{5,4},{6,5},{7,6},{9,8},{10,9},{11,10},{12... | collective-permute-start | bytes 196616 | tf_op jit(solution)/shard_map/ppermute | solution.py:170
  70.6 2.2 %copy-start.11 = (bf16[2,256,256]{2,1,0:T(8,128)(2,1)S(1)}, bf16[2,256,256]{2,1,0:T(8,128)(2,1)}, u32[]{:S(2)}) copy-start(bf16[2,256,256]{2,1,0:T(8,128)(2,1)} %param.38) | copy-start | bytes 786436

commit v2 on v1

--- a/solution.py
+++ b/solution.py
@@ -170,33 +170,172 @@
             lax.ppermute(edge_rows[:rim], "dom", backward))
 
 
-def layer_norm_rows(values):
-    row_mean = jnp.mean(values, axis=-1, keepdims=True)
-    centred = values - row_mean
-    variance = jnp.mean(centred * centred, axis=-1, keepdims=True)
-    return centred * lax.rsqrt(variance + EPSILON)
-
-
-def edge_node(
-    sender_proj, own_rows, edge_rows, senders, edge_in, edge_out, node_in, node_out, biases, gains
+def coarse_kernel(
+    part, lat, edge, sends, lists, ein, eout, nin, nout, bias, gain,
+    out,
+    got, edges_lo, edges_hi, rim_out, rim_in, mix, sum_send, sum_recv, rim_send, rim_recv,
 ):
-    node_count = own_rows.shape[0]
-    width = own_rows.shape[1]
-    fanin = edge_rows.shape[0] // node_count
-    receiver_proj = dot(own_rows, edge_in[1])
-    edge_pre = dot(edge_rows, edge_in[2])
-    edge_pre = edge_pre + sender_proj[senders].astype(F32) + biases[0]
-    edge_pre = (edge_pre.reshape(node_count, fanin, width) + receiver_proj[:, None, :]).reshape(
-        node_count * fanin, width
+    groups = part.shape[0]
+    rows, width = lat.shape
+    rim = rim_in.shape[1]
+    mine = lax.axis_index("group")
+    here = lax.axis_index("dom")
+    last = lax.axis_size("dom") - 1
+    has_low = here > 0
+    has_high = here < last
+    below = jnp.maximum(here - 1, 0)
+    above = jnp.minimum(here + 1, last)
+    mesh_id = pl.DeviceIdType.MESH
+
+    barrier = pltpu.get_barrier_semaphore()
+    for o in range(1, groups):
+        pl.semaphore_signal(
+            barrier, inc=1, device_id=(lax.rem(mine + o, groups), here), device_id_type=mesh_id
+        )
+
+    @pl.when(has_low)
+    def _():
+        pl.semaphore_signal(barrier, inc=1, device_id=(mine, below), device_id_type=mesh_id)
+
+    @pl.when(has_high)
+    def _():
+        pl.semaphore_signal(barrier, inc=1, device_id=(mine, above), device_id_type=mesh_id)
+
+    pl.semaphore_wait(barrier, groups - 1 + has_low.astype(jnp.int32) + has_high.astype(jnp.int32))
+    copies = []
+    for o in range(1, groups):
+        peer = lax.rem(mine + o, groups)
+        copy = pltpu.make_async_remote_copy(
+            src_ref=part.at[peer], dst_ref=got.at[o - 1],
+            send_sem=sum_send.at[o - 1], recv_sem=sum_recv.at[o - 1],
+            device_id=(peer, here), device_id_type=mesh_id,
+        )
+        copy.start()
+        copies.append(copy)
+
+    eoc = centre(eout[...])
+    noc = centre(nout[...])
+    b = bias[...]
+    bc = b - jnp.mean(b, axis=-1, keepdims=True)
+    for r in range(0, edge.shape[0], 256):
+        p = dot(edge[r:r + 256, :], ein[2])
+        edges_lo[r:r + 256, :] = p[:, :128]
+        edges_hi[r:r + 256, :] = p[:, 128:]
+    sums = part[mine].astype(F32)
+    for copy in copies:
+        copy.wait_recv()
+    for o in range(1, groups):
+        sums = sums + got[o - 1].astype(F32)
+    members = sums[rows:rows + 1, :] + sums[rows + 1:rows + 2, :]
+    inv = jnp.broadcast_to(1.0 / jnp.maximum(members, 1.0), (128, rows)).T
+    inv = jnp.concatenate([inv] * (width // 128), axis=1)
+    own = (lat[...].astype(F32) + sums[:rows, :] * inv).astype(BF16)
+    names = lax.broadcasted_iota(jnp.int32, (2 * rim, rows), 1)
+    chosen = jnp.where(names == lists[...], 1.0, 0.0).astype(BF16)
+    border_rows = dot(chosen, own).astype(BF16)
+    rim_out[0] = border_rows[:rim, :]
+    rim_out[1] = border_rows[rim:, :]
+    down = pltpu.make_async_remote_copy(
+        src_ref=rim_out.at[0], dst_ref=rim_in.at[1],
+        send_sem=rim_send.at[0], recv_sem=rim_recv.at[0],
+        device_id=(mine, below), device_id_type=mesh_id,
     )
-    edge_hidden = jnp.maximum(edge_pre, 0.0).astype(BF16)
-    message = layer_norm_rows(dot(edge_hidden, edge_out) + biases[1]) * gains[0]
-    message = message.astype(BF16)
-    summed = jnp.sum(message.astype(F32).reshape(node_count, fanin, width), axis=1).astype(BF16)
-    node_pre = dot(own_rows, node_in[0]) + dot(summed, node_in[1]) + biases[2]
-    node_hidden = jnp.maximum(node_pre, 0.0).astype(BF16)
-    update = layer_norm_rows(dot(node_hidden, node_out) + biases[3]) * gains[1]
-    return (own_rows.astype(F32) + update).astype(BF16)
+    up = pltpu.make_async_remote_copy(
+        src_ref=rim_out.at[1], dst_ref=rim_in.at[0],
+        send_sem=rim_send.at[1], recv_sem=rim_recv.at[1],
+        device_id=(mine, above), device_id_type=mesh_id,
+    )
+
+    @pl.when(has_low)
+    def _():
+        down.start()
+
+    @pl.when(has_high)
+    def _():
+        up.start()
+
+    @pl.when(jnp.logical_not(has_low))
+    def _():
+        rim_in[0] = jnp.zeros((rim, width), BF16)
+
+    @pl.when(jnp.logical_not(has_high))
+    def _():
+        rim_in[1] = jnp.zeros((rim, width), BF16)
+
+    sender = dot(own, ein[0]).astype(BF16)
+    recv = dot(own, ein[1]) + b[0:1, :]
+    npre = dot(own, nin[0]) + b[2:3, :]
+    inner = lax.broadcasted_iota(jnp.int32, (rows, rows), 1) + rim
+    outer = lax.broadcasted_iota(jnp.int32, (rows, 2 * rim), 1)
+    outer = outer + jnp.where(outer >= rim, rows, 0)
+    for k in range(DEG):
+        member = jnp.where(inner == sends[:, k:k + 1], 1.0, 0.0).astype(BF16)
+        e = jnp.concatenate(
+            [edges_lo[pl.ds(k, rows, stride=DEG), :], edges_hi[pl.ds(k, rows, stride=DEG), :]],
+            axis=1,
+        )
+        mix[k] = e + recv + dot(member, sender)
+
+    @pl.when(has_high)
+    def _():
+        down.wait_recv()
+
+    @pl.when(has_low)
+    def _():
+        up.wait_recv()
+
+    low = dot(rim_in[0], ein[0]).astype(BF16)
+    high = dot(rim_in[1], ein[0]).astype(BF16)
+    rims = jnp.concatenate([low, high], axis=0)
+    total = jnp.zeros((rows, width), F32)
+    for k in range(DEG):
+        member = jnp.where(outer == sends[:, k:k + 1], 1.0, 0.0).astype(BF16)
+        h = jnp.maximum(mix[k] + dot(member, rims), 0.0).astype(BF16)
+        total = total + unit_rows(dot(h, eoc) + bc[1:2, :])
+    summed = (total * gain[0:1, :]).astype(BF16)
+    h = jnp.maximum(npre + dot(summed, nin[1]), 0.0).astype(BF16)
+    update = unit_rows(dot(h, noc) + bc[3:4, :]) * gain[1:2, :]
+    out[...] = (own.astype(F32) + update).astype(BF16)
+    for copy in copies:
+        copy.wait_send()
+
+    @pl.when(has_low)
+    def _():
+        down.wait_send()
+
+    @pl.when(has_high)
+    def _():
+        up.wait_send()
+
+
+def coarse_level(part, lat, edge, send, lists, ein, eout, nin, nout, bias, gain):
+    groups = part.shape[0]
+    rows, width = lat.shape
+    rim = lists.shape[0] // 2
+    return pl.pallas_call(
+        coarse_kernel,
+        in_specs=[pl.BlockSpec(memory_space=pltpu.VMEM)] * 11,
+        out_specs=pl.BlockSpec(memory_space=pltpu.VMEM),
+        out_shape=jax.ShapeDtypeStruct((rows, width), BF16),
+        scratch_shapes=[
+            pltpu.VMEM((groups - 1,) + part.shape[1:], BF16),
+            pltpu.VMEM((edge.shape[0], 128), F32),
+            pltpu.VMEM((edge.shape[0], 128), F32),
+            pltpu.VMEM((2, rim, width), BF16),
+            pltpu.VMEM((2, rim, width), BF16),
+            pltpu.VMEM((DEG, rows, width), F32),
+            pltpu.SemaphoreType.DMA((groups - 1,)),
+            pltpu.SemaphoreType.DMA((groups - 1,)),
+            pltpu.SemaphoreType.DMA((2,)),
+            pltpu.SemaphoreType.DMA((2,)),
+        ],
+        compiler_params=pltpu.CompilerParams(
+            vmem_limit_bytes=32 * 1024 * 1024, collective_id=0, has_side_effects=True
+        ),
+        cost_estimate=pl.CostEstimate(flops=1_500_000_000, bytes_accessed=3_000_000, transcendentals=0),
+        name="coarse_level",
+    )(part, lat, edge, send.reshape(rows, DEG), lists.reshape(2 * rim, 1),
+      ein, eout, nin, nout, bias, gain)
 
 
 def body(
@@ -213,18 +352,8 @@
         groups, clusters, edge_send, pool_id, node_lat, low, high, edge_lat,
         fine_edge_in, fine_edge_out, fine_node_in, fine_node_out, fine_bias, fine_gain,
     )
-    got = lax.all_to_all(part, "group", split_axis=0, concat_axis=0, tiled=True).astype(F32)
-    got = got.sum(axis=0)
-    cluster_sum = got[:clusters]
-    member_count = got[clusters] + got[clusters + 1]
-    pooled_mean = cluster_sum / jnp.maximum(member_count, 1.0)[:, None]
-    coarse_in = (coarse_lat.astype(F32) + pooled_mean).astype(BF16)
-    crim = chalo_list.shape[0] // 2
-    clow, chigh = exchange(border(coarse_in, chalo_list), crim)
-    cext = jnp.concatenate([clow, coarse_in, chigh], axis=0)
-    coarse_out = edge_node(
-        dot(cext, coarse_edge_in[0]).astype(BF16),
-        coarse_in, cedge_lat, cedge_send,
+    coarse_out = coarse_level(
+        part, coarse_lat, cedge_lat, cedge_send, chalo_list,
         coarse_edge_in, coarse_edge_out, coarse_node_in, coarse_node_out, coarse_bias, coarse_gain,
     )
     return (fine_out, coarse_out)

time: 75.5 us -> 57.2 us (0.76)
  Pallas kernels: 26.1 us -> 40.2 us
  starting transfers between devices: 17.6 us -> 6.52 us
  local copies, waits for them, and re-layouts: 8.74 us -> 1.05 us
  matrix products: 8.51 us -> 2.83 us
  waiting for transfers between devices: 10.8 us -> 5.46 us
  other arithmetic: 2.36 us -> 0 us
    pallas_call x0 -> x1, Pallas kernels: none -> 14.3 us  [coarse_level(): pl.pallas_call(coarse_kernel, in_specs=[pl.BlockSpec(memory_space=pltpu.V...]
    dot_general x7 -> x1, matrix products: 8.51 us -> 2.83 us  [dot(): return jnp.dot(a, b, preferred_element_type=F32)]
    ppermute x2 -> x1, starting transfers between devices: 10.2 us -> 4.6 us  [exchange(): lax.ppermute(edge_rows[rim:], 'dom', forward)]
    all_to_all x1 -> x0, waiting for transfers between devices: 4.44 us -> none  [body(): lax.all_to_all(part, 'group', split_axis=0, concat_axis=0, tiled=True)]
    gather x1 -> x0, local copies, waits for them, and re-layouts: 3.94 us -> none  [edge_node(): edge_pre = edge_pre + sender_proj[senders].astype(F32) + biases[0]]
    all_to_all x1 -> x0, starting transfers between devices: 3.61 us -> none  [body(): lax.all_to_all(part, 'group', split_axis=0, concat_axis=0, tiled=True)]
    ppermute x2 -> x1, starting transfers between devices: 3.84 us -> 1.92 us  [exchange(): lax.ppermute(edge_rows[:rim], 'dom', backward)]
    ppermute x2 -> x1, waiting for transfers between devices: 5.68 us -> 4.4 us  [exchange(): lax.ppermute(edge_rows[:rim], 'dom', backward)]
  transfers between devices with their start and end apart: 5 -> 2, of which waited for: 4 -> 2; matrix products, arithmetic and copies ran while one was open for 6% -> 0% of each run, Pallas kernels for 0% -> 0%
where the time goes in v2:
time: 57.2 us; the launch traced here: 57 us
  Pallas kernels  40.2 us (70%)
  starting transfers between devices  6.52 us (11%)
  waiting for transfers between devices  5.46 us (10%)
  matrix products  2.83 us (5%)
  local copies, waits for them, and re-layouts  1.05 us (2%)
  between operations  0.95 us (2%)
    pallas_call x1, Pallas kernels, fine_level(): pl.pallas_call(functools.partial(fine_kernel, groups, clusters), grid=(st...  25.8 us
    pallas_call x1, Pallas kernels, coarse_level(): pl.pallas_call(coarse_kernel, in_specs=[pl.BlockSpec(memory_space=pltpu.V...  14.3 us
    ppermute x1, starting transfers between devices, exchange(): lax.ppermute(edge_rows[rim:], 'dom', forward)  4.6 us
    ppermute x1, waiting for transfers between devices, exchange(): lax.ppermute(edge_rows[:rim], 'dom', backward)  4.4 us
    dot_general x1, matrix products, dot(): return jnp.dot(a, b, preferred_element_type=F32)  2.83 us
    ppermute x1, starting transfers between devices, exchange(): lax.ppermute(edge_rows[:rim], 'dom', backward)  1.92 us
  transfers between devices with their start and end apart: 2, of which 2 were waited for; matrix products, arithmetic and copies ran while one was open for 0% of the time, Pallas kernels for 0%

profile of v2, /device:TPU:1, one launch (start us, length us, event | category | flops | bytes accessed | tf_op | source)
XLA Modules:
  0.0 57.0 jit_solution(15417101529923737744)
XLA Ops:
  0.6 0.0 copy-start
  0.6 0.0 copy-start.18
  0.7 0.0 copy-start.17
  0.7 0.0 copy-start.12
  0.7 0.0 copy-start.11
  0.7 0.0 copy-start.2
  0.7 2.8 %fusion.2 = bf16[1024,256]{1,0:T(8,128)(2,1)S(1)} fusion(bf16[2048,256]{1,0:T(8,128)(2,1)} %node.1, s32[1024]{0:T(1024)} %param.24), kind=kOutput, calls=%fused_computation.3 | convolution fusion | flops 1076101120 | bytes 1576960 | tf_op jit(solution)/shard_map/dot_general | solution.py:18
  3.6 4.6 %collective-permute-start = (bf16[512,256]{1,0:T(8,128)(2,1)S(1)}, bf16[512,256]{1,0:T(8,128)(2,1)S(1)}, u32[]{:S(2)}, u32[]{:S(2)}) collective-permute-start(bf16[512,256]{1,0:T(8,128)(2,1)S(1)} %get-tuple-element.7), channel_id=1, source_target_pairs={{0,1},{1,2},{2,3},{3,4},{4,5},{5,6},{6,7},{8,9},{9,10},{10,11},{11... | collective-permute-start | bytes 786440 | tf_op jit(solution)/shard_map/ppermute | solution.py:169
  8.2 1.9 %collective-permute-start.1 = (bf16[512,256]{1,0:T(8,128)(2,1)S(1)}, bf16[512,256]{1,0:T(8,128)(2,1)S(1)}, u32[]{:S(2)}, u32[]{:S(2)}) collective-permute-start(bf16[512,256]{1,0:T(8,128)(2,1)S(1)} %get-tuple-element.6), channel_id=1, source_target_pairs={{1,0},{2,1},{3,2},{4,3},{5,4},{6,5},{7,6},{9,8},{10,9},{11,10},{12... | collective-permute-start | bytes 786440 | tf_op jit(solution)/shard_map/ppermute | solution.py:170
  10.2 0.1 copy.23.lists
  10.3 0.1 reshape.15.sends
  10.5 1.1 %collective-permute-done.low = bf16[512,256]{1,0:T(8,128)(2,1)S(1)} collective-permute-done((bf16[512,256]{1,0:T(8,128)(2,1)S(1)}, bf16[512,256]{1,0:T(8,128)(2,1)S(1)}, u32[]{:S(2)}, u32[]{:S(2)}) %collective-permute-start) | collective-permute-done | bytes 262176 | tf_op jit(solution)/shard_map/ppermute | solution.py:169
  11.5 4.4 %collective-permute-done.1.high = bf16[512,256]{1,0:T(8,128)(2,1)S(1)} collective-permute-done((bf16[512,256]{1,0:T(8,128)(2,1)S(1)}, bf16[512,256]{1,0:T(8,128)(2,1)S(1)}, u32[]{:S(2)}, u32[]{:S(2)}) %collective-permute-start.1) | collective-permute-done | bytes 262176 | tf_op jit(solution)/shard_map/ppermute | solution.py:170
  16.0 0.0 copy-start.1
  16.0 0.0 copy-start.3
  16.0 0.0 copy-start.5
  16.0 0.0 copy-start.8
  16.0 0.0 copy-start.9
  16.1 0.0 copy-start.10
  16.1 0.0 copy-start.14
  16.1 0.0 copy-start.16
  16.1 25.8 %fine_level.1 = (bf16[2048,256]{1,0:T(8,128)(2,1)}, bf16[4,272,256]{2,1,0:T(8,128)(2,1)S(1)}) custom-call(s32[8192]{0:T(1024)S(1)} %copy-done.11, s32[16,128]{1,0:T(8,128)S(1)} %bitcast.3, bf16[2048,256]{1,0:T(8,128)(2,1)S(1)} %copy-done, bf16[512,256]{1,0:T(8,128)(2,1)S(1)} %collective-permute-done.low, bf16[512,256]{1,0:T(8,128)(2,1)S(1)} %collective-permute-done.1.high, ...), custom_call_target="tpu_custom_call" | custom-call | flops 7000000000 | bytes 9000000 | tf_op jit(solution)/shard_map/fine_level/pallas_call | solution.py:130
  42.0 14.3 %coarse_level.1 = bf16[256,256]{1,0:T(8,128)(2,1)S(1)} custom-call(bf16[4,272,256]{2,1,0:T(8,128)(2,1)S(1)} %get-tuple-element.5.part, bf16[256,256]{1,0:T(8,128)(2,1)S(1)} %copy-done.8, bf16[1024,256]{1,0:T(8,128)(2,1)S(1)} %copy-done.1, s32[256,4]{1,0:T(8,128)S(1)} %reshape.15.sends, s32[256,1]{1,0:T(8,128)S(1)} %copy.23.lists, ...), custom_call_target="tpu_custom_call" | custom-call | flops 1500000000 | bytes 3000000 | tf_op jit(solution)/shard_map/coarse_level/pallas_call | solution.py:315
  56.3 0.7 %copy.25 = bf16[256,256]{1,0:T(8,128)(2,1)} copy(bf16[256,256]{1,0:T(8,128)(2,1)S(1)} %coarse_level.1) | data formatting | bytes 262144
  (25 shorter events, 0.1 us)
Async XLA Ops:
  0.6 15.3 %copy-start = (bf16[2048,256]{1,0:T(8,128)(2,1)S(1)}, bf16[2048,256]{1,0:T(8,128)(2,1)}, u32[]{:S(2)}) copy-start(bf16[2048,256]{1,0:T(8,128)(2,1)} %node.1) | copy-start | bytes 3145732
  0.6 9.5 %copy-start.18 = (s32[256]{0:T(256)S(1)}, s32[256]{0:T(256)}, u32[]{:S(2)}) copy-start(s32[256]{0:T(256)} %param.29) | copy-start | bytes 3076
  0.7 9.7 %copy-start.17 = (s32[1024]{0:T(1024)S(1)}, s32[1024]{0:T(1024)}, u32[]{:S(2)}) copy-start(s32[1024]{0:T(1024)} %param.28) | copy-start | bytes 12292
  0.7 15.3 %copy-start.12 = (s32[2048]{0:T(1024)S(1)}, s32[2048]{0:T(1024)}, u32[]{:S(2)}) copy-start(s32[2048]{0:T(1024)} %param.25) | copy-start | bytes 24580
  0.7 15.3 %copy-start.11 = (s32[8192]{0:T(1024)S(1)}, s32[8192]{0:T(1024)}, u32[]{:S(2)}) copy-start(s32[8192]{0:T(1024)} %send.1) | copy-start | bytes 98308
  0.7 15.3 %copy-start.2 = (bf16[3,256,256]{2,1,0:T(8,128)(2,1)S(1)}, bf16[3,256,256]{2,1,0:T(8,128)(2,1)}, u32[]{:S(2)}) copy-start(bf16[3,256,256]{2,1,0:T(8,128)(2,1)} %ein.2) | copy-start | bytes 1179652
  0.7 15.3 %copy-start.6 = (bf16[256,256]{1,0:T(8,128)(2,1)S(1)}, bf16[256,256]{1,0:T(8,128)(2,1)}, u32[]{:S(2)}) copy-start(bf16[256,256]{1,0:T(8,128)(2,1)} %eout.2) | copy-start | bytes 393220
  0.7 15.3 %copy-start.4 = (bf16[2,256,256]{2,1,0:T(8,128)(2,1)S(1)}, bf16[2,256,256]{2,1,0:T(8,128)(2,1)}, u32[]{:S(2)}) copy-start(bf16[2,256,256]{2,1,0:T(8,128)(2,1)} %nin.2) | copy-start | bytes 786436
  0.7 15.3 %copy-start.7 = (bf16[256,256]{1,0:T(8,128)(2,1)S(1)}, bf16[256,256]{1,0:T(8,128)(2,1)}, u32[]{:S(2)}) copy-start(bf16[256,256]{1,0:T(8,128)(2,1)} %nout.2) | copy-start | bytes 393220
  0.7 15.3 %copy-start.13 = (f32[4,256]{1,0:T(4,128)S(1)}, f32[4,256]{1,0:T(4,128)}, u32[]{:S(2)}) copy-start(f32[4,256]{1,0:T(4,128)} %bias.2) | copy-start | bytes 12292
  0.7 15.3 %copy-start.15 = (f32[2,256]{1,0:T(2,128)S(1)}, f32[2,256]{1,0:T(2,128)}, u32[]{:S(2)}) copy-start(f32[2,256]{1,0:T(2,128)} %gain.2) | copy-start | bytes 6148
  3.6 7.9 %collective-permute-start = (bf16[512,256]{1,0:T(8,128)(2,1)S(1)}, bf16[512,256]{1,0:T(8,128)(2,1)S(1)}, u32[]{:S(2)}, u32[]{:S(2)}) collective-permute-start(bf16[512,256]{1,0:T(8,128)(2,1)S(1)} %get-tuple-element.7), channel_id=1, source_target_pairs={{0,1},{1,2},{2,3},{3,4},{4,5},{5,6},{6,7},{8,9},{9,10},{10,11},{11... | collective-permute-start | bytes 786440 | tf_op jit(solution)/shard_map/ppermute | solution.py:169
  8.2 7.7 %collective-permute-start.1 = (bf16[512,256]{1,0:T(8,128)(2,1)S(1)}, bf16[512,256]{1,0:T(8,128)(2,1)S(1)}, u32[]{:S(2)}, u32[]{:S(2)}) collective-permute-start(bf16[512,256]{1,0:T(8,128)(2,1)S(1)} %get-tuple-element.6), channel_id=1, source_target_pairs={{1,0},{2,1},{3,2},{4,3},{5,4},{6,5},{7,6},{9,8},{10,9},{11,10},{12... | collective-permute-start | bytes 786440 | tf_op jit(solution)/shard_map/ppermute | solution.py:170
  16.0 25.9 %copy-start.1 = (bf16[1024,256]{1,0:T(8,128)(2,1)S(1)}, bf16[1024,256]{1,0:T(8,128)(2,1)}, u32[]{:S(2)}) copy-start(bf16[1024,256]{1,0:T(8,128)(2,1)} %edge.3) | copy-start | bytes 1572868
  16.0 25.9 %copy-start.3 = (bf16[3,256,256]{2,1,0:T(8,128)(2,1)S(1)}, bf16[3,256,256]{2,1,0:T(8,128)(2,1)}, u32[]{:S(2)}) copy-start(bf16[3,256,256]{2,1,0:T(8,128)(2,1)} %ein.3) | copy-start | bytes 1179652
  16.0 25.9 %copy-start.5 = (bf16[2,256,256]{2,1,0:T(8,128)(2,1)S(1)}, bf16[2,256,256]{2,1,0:T(8,128)(2,1)}, u32[]{:S(2)}) copy-start(bf16[2,256,256]{2,1,0:T(8,128)(2,1)} %nin.3) | copy-start | bytes 786436
  16.0 25.9 %copy-start.8 = (bf16[256,256]{1,0:T(8,128)(2,1)S(1)}, bf16[256,256]{1,0:T(8,128)(2,1)}, u32[]{:S(2)}) copy-start(bf16[256,256]{1,0:T(8,128)(2,1)} %lat.1) | copy-start | bytes 393220
  16.0 25.9 %copy-start.9 = (bf16[256,256]{1,0:T(8,128)(2,1)S(1)}, bf16[256,256]{1,0:T(8,128)(2,1)}, u32[]{:S(2)}) copy-start(bf16[256,256]{1,0:T(8,128)(2,1)} %eout.3) | copy-start | bytes 393220
  16.1 25.9 %copy-start.10 = (bf16[256,256]{1,0:T(8,128)(2,1)S(1)}, bf16[256,256]{1,0:T(8,128)(2,1)}, u32[]{:S(2)}) copy-start(bf16[256,256]{1,0:T(8,128)(2,1)} %nout.3) | copy-start | bytes 393220
  16.1 25.9 %copy-start.14 = (f32[4,256]{1,0:T(4,128)S(1)}, f32[4,256]{1,0:T(4,128)}, u32[]{:S(2)}) copy-start(f32[4,256]{1,0:T(4,128)} %bias.3) | copy-start | bytes 12292
  16.1 25.9 %copy-start.16 = (f32[2,256]{1,0:T(2,128)S(1)}, f32[2,256]{1,0:T(2,128)}, u32[]{:S(2)}) copy-start(f32[2,256]{1,0:T(2,128)} %gain.3) | copy-start | bytes 6148

commit v3 on v2

--- a/solution.py
+++ b/solution.py
@@ -10,7 +10,7 @@
 EPSILON = 1e-05
 F32 = jnp.float32
 BF16 = jnp.bfloat16
-NT = 128
+NT = 256
 DEG = 4
 
 
@@ -27,21 +27,154 @@
     return z * lax.rsqrt(jnp.mean(z * z, axis=-1, keepdims=True) + EPSILON)
 
 
+def column(row):
+    return jnp.broadcast_to(row, (128, 128)).T
+
+
+def neighbours():
+    here = lax.axis_index("dom")
+    last = lax.axis_size("dom") - 1
+    return here > 0, here < last, jnp.maximum(here - 1, 0), jnp.minimum(here + 1, last)
+
+
+def rim_copies(rim_out, rim_in, rim_send, rim_recv, below, above):
+    mine = lax.axis_index("group")
+    return tuple(
+        pltpu.make_async_remote_copy(
+            src_ref=rim_out.at[i], dst_ref=rim_in.at[1 - i],
+            send_sem=rim_send.at[i], recv_sem=rim_recv.at[i],
+            device_id=(mine, to), device_id_type=pl.DeviceIdType.MESH,
+        )
+        for i, to in enumerate((below, above))
+    )
+
+
+def front_kernel(
+    lists, node, ein, table, scale, proj, rim_out, rim_in, rim_send, rim_recv
+):
+    rows, width = node.shape
+    rim = rim_in.shape[1]
+    mine = lax.axis_index("group")
+    has_low, has_high, below, above = neighbours()
+    barrier = pltpu.get_barrier_semaphore()
+
+    @pl.when(has_low)
+    def _():
+        pl.semaphore_signal(
+            barrier, inc=1, device_id=(mine, below), device_id_type=pl.DeviceIdType.MESH
+        )
+
+    @pl.when(has_high)
+    def _():
+        pl.semaphore_signal(
+            barrier, inc=1, device_id=(mine, above), device_id_type=pl.DeviceIdType.MESH
+        )
+
+    @pl.when(jnp.logical_not(has_low))
+    def _():
+        rim_in[0] = jnp.zeros((rim, width), BF16)
+
+    @pl.when(jnp.logical_not(has_high))
+    def _():
+        rim_in[1] = jnp.zeros((rim, width), BF16)
+
+    down, up = rim_copies(rim_out, rim_in, rim_send, rim_recv, below, above)
+    lane = lax.broadcasted_iota(jnp.int32, (128, 128), 1)
+
+    def pick(side):
+        for r in range(0, rim, 128):
+            at = (side * rim + r) // 128
+            names = column(lists[at:at + 1, :])
+            chosen = jnp.concatenate(
+                [jnp.where(names == lane + j, 1.0, 0.0).astype(BF16) for j in range(0, rows, 128)],
+                axis=1,
+            )
+            rim_out[side, r:r + 128, :] = dot(chosen, node[...]).astype(BF16)
+
+    pick(0)
+    pl.semaphore_wait(barrier, has_low.astype(jnp.int32) + has_high.astype(jnp.int32))
+
+    @pl.when(has_low)
+    def _():
+        down.start()
+
+    pick(1)
+
+    @pl.when(has_high)
+    def _():
+        up.start()
+
+    top = jnp.full((1, width), 1e-20, F32)
+    for r in range(0, rows, 256):
+        p = dot(node[r:r + 256, :], ein[0])
+        proj[rim + r:rim + r + 256, :] = p
+        top = jnp.maximum(top, jnp.max(jnp.abs(p), axis=0, keepdims=True))
+
+    @pl.when(has_high)
+    def _():
+        down.wait_recv()
+
+    @pl.when(has_low)
+    def _():
+        up.wait_recv()
+
+    for side, start in ((0, 0), (1, rim + rows)):
+        for r in range(0, rim, 256):
+            p = dot(rim_in[side, r:r + 256, :], ein[0])
+            proj[start + r:start + r + 256, :] = p
+            top = jnp.maximum(top, jnp.max(jnp.abs(p), axis=0, keepdims=True))
+    scale[...] = top * (1.0 / 32767.0)
+    inv = 32767.0 / top
+    for r in range(0, rows + 2 * rim, 256):
+        q = jnp.round(proj[r:r + 256, :] * inv).astype(jnp.int32)
+        table[r:r + 256, :] = (q[:, :128] & 0xFFFF) | (q[:, 128:] << 16)
+
+    @pl.when(has_low)
+    def _():
+        down.wait_send()
+
+    @pl.when(has_high)
+    def _():
+        up.wait_send()
+
+
+def front(lists, node, ein):
+    rows, width = node.shape
+    rim = lists.shape[0] // 2
+    return pl.pallas_call(
+        front_kernel,
+        in_specs=[pl.BlockSpec(memory_space=pltpu.VMEM)] * 3,
+        out_specs=[pl.BlockSpec(memory_space=pltpu.VMEM)] * 2,
+        out_shape=[jax.ShapeDtypeStruct((rows + 2 * rim, 128), jnp.int32),
+                   jax.ShapeDtypeStruct((1, width), F32)],
+        scratch_shapes=[
+            pltpu.VMEM((rows + 2 * rim, width), F32),
+            pltpu.VMEM((2, rim, width), BF16),
+            pltpu.VMEM((2, rim, width), BF16),
+            pltpu.SemaphoreType.DMA((2,)),
+            pltpu.SemaphoreType.DMA((2,)),
+        ],
+        compiler_params=pltpu.CompilerParams(
+            vmem_limit_bytes=32 * 1024 * 1024, collective_id=1, has_side_effects=True
+        ),
+        cost_estimate=pl.CostEstimate(flops=1_500_000_000, bytes_accessed=3_000_000, transcendentals=0),
+        name="front",
+    )(lists.reshape(2 * rim // 128, 128), node, ein)
+
+
 def fine_kernel(
     groups, clusters,
-    send, pool, node, low, high, edge, ein, eout, nin, nout, bias, gain,
+    send, pool, table, scale, node, edge, ein, eout, nin, nout, bias, gain,
     out, part,
-    table, proj, scale, gath, pre_lo, pre_hi, recv, npre, eoc, noc, bc, acc, cnt,
+    gath, pre_lo, pre_hi, eoc, noc, bc, acc, cnt,
 ):
     step = pl.program_id(0)
     steps = pl.num_programs(0)
-    rows = node.shape[0]
-    rim = low.shape[0]
     et = NT * DEG
 
     def fetch(tile, k, n):
         at = send[tile * et + n * DEG + k]
-        gath[pl.ds(k * NT + n, 1), :] = table[pl.ds(at, 1), :]
+        gath[pl.ds(k * NT + n, 1), :] = table[at]
 
     @pl.when(step == 0)
     def _():
@@ -49,22 +182,6 @@
         noc[...] = centre(nout[...])
         b = bias[...]
         bc[...] = b - jnp.mean(b, axis=-1, keepdims=True)
-        top = jnp.zeros((1, 256), F32)
-        for ref, start in ((low, 0), (node, rim), (high, rim + rows)):
-            for r in range(0, ref.shape[0], 256):
-                p = dot(ref[r:r + 256, :], ein[0])
-                proj[start + r:start + r + 256, :] = p
-                top = jnp.maximum(top, jnp.max(jnp.abs(p), axis=0, keepdims=True))
-        top = jnp.maximum(top, 1e-20)
-        scale[...] = top * (1.0 / 32767.0)
-        inv = 32767.0 / top
-        for r in range(0, rows + 2 * rim, 256):
-            q = jnp.round(proj[r:r + 256, :] * inv).astype(jnp.int32)
-            table[r:r + 256, :] = (q[:, :128] & 0xFFFF) | (q[:, 128:] << 16)
-        for r in range(0, rows, 256):
-            own = node[r:r + 256, :]
-            recv[r:r + 256, :] = dot(own, ein[1]) + bias[0:1, :]
-            npre[r:r + 256, :] = dot(own, nin[0]) + bias[2:3, :]
         acc[...] = jnp.zeros_like(acc)
         cnt[...] = jnp.zeros_like(cnt)
 
@@ -75,12 +192,12 @@
 
         lax.fori_loop(0, NT, first, 0, unroll=8)
 
-    base = pl.multiple_of(step * NT, NT)
     nxt = jnp.minimum(step + 1, steps - 1)
     p = dot(edge[...], ein[2])
     pre_lo[...] = p[:, :128]
     pre_hi[...] = p[:, 128:]
-    rv = recv[pl.ds(base, NT), :]
+    own = node[...]
+    rv = dot(own, ein[1]) + bias[0:1, :]
     total = jnp.zeros((NT, 256), F32)
     for k in range(DEG):
         g = gath[k * NT:(k + 1) * NT, :]
@@ -93,9 +210,9 @@
         for n in range(NT):
             fetch(nxt, k, n)
     summed = (total * gain[0:1, :]).astype(BF16)
-    h = jnp.maximum(npre[pl.ds(base, NT), :] + dot(summed, nin[1]), 0.0).astype(BF16)
+    h = jnp.maximum(dot(own, nin[0]) + dot(summed, nin[1]) + bias[2:3, :], 0.0).astype(BF16)
     update = unit_rows(dot(h, noc[...]) + bc[3:4, :]) * gain[1:2, :]
-    result = (node[pl.ds(base, NT), :].astype(F32) + update).astype(BF16)
+    result = (own.astype(F32) + update).astype(BF16)
     out[...] = result
     ids = pool[pl.ds(step, 1), :]
     ones = jnp.ones((16, NT), BF16)
@@ -121,30 +238,25 @@
             ).astype(BF16)
 
 
-def fine_level(groups, clusters, send, pool, node, low, high, edge, ein, eout, nin, nout, bias, gain):
+def fine_level(groups, clusters, send, pool, table, scale, node, edge, ein, eout, nin, nout, bias, gain):
     rows, width = node.shape
-    rim = low.shape[0]
     steps = rows // NT
     et = NT * DEG
     whole = pl.BlockSpec(memory_space=pltpu.VMEM)
     return pl.pallas_call(
         functools.partial(fine_kernel, groups, clusters),
         grid=(steps,),
-        in_specs=[pl.BlockSpec(memory_space=pltpu.SMEM), whole, whole, whole, whole,
+        in_specs=[pl.BlockSpec(memory_space=pltpu.SMEM), whole, whole, whole,
+                  pl.BlockSpec((NT, width), lambda i: (i, 0)),
                   pl.BlockSpec((et, width), lambda i: (i, 0))] + [whole] * 6,
         out_specs=[pl.BlockSpec((NT, width), lambda i: (i, 0)),
                    pl.BlockSpec((groups, clusters + 16, width), lambda i: (0, 0, 0))],
         out_shape=[jax.ShapeDtypeStruct((rows, width), BF16),
                    jax.ShapeDtypeStruct((groups, clusters + 16, width), BF16)],
         scratch_shapes=[
-            pltpu.VMEM((rows + 2 * rim, 128), jnp.int32),
-            pltpu.VMEM((rows + 2 * rim, width), F32),
-            pltpu.VMEM((1, width), F32),
             pltpu.VMEM((et, 128), jnp.int32),
             pltpu.VMEM((et, 128), F32),
             pltpu.VMEM((et, 128), F32),
-            pltpu.VMEM((rows, width), F32),
-            pltpu.VMEM((rows, width), F32),
             pltpu.VMEM((width, width), BF16),
             pltpu.VMEM((width, width), BF16),
             pltpu.VMEM((4, width), F32),
@@ -154,20 +266,7 @@
         compiler_params=pltpu.CompilerParams(vmem_limit_bytes=48 * 1024 * 1024),
         cost_estimate=pl.CostEstimate(flops=7_000_000_000, bytes_accessed=9_000_000, transcendentals=0),
         name="fine_level",
-    )(send, pool.reshape(steps, NT), node, low, high, edge, ein, eout, nin, nout, bias, gain)
-
-
-def border(rows, chosen):
-    table = (chosen[:, None] == jnp.arange(rows.shape[0], dtype=jnp.int32)[None, :]).astype(BF16)
-    return dot(table, rows).astype(BF16)
-
-
-def exchange(edge_rows, rim):
-    count = lax.axis_size("dom")
-    forward = [(i, i + 1) for i in range(count - 1)]
-    backward = [(t, s) for s, t in forward]
-    return (lax.ppermute(edge_rows[rim:], "dom", forward),
-            lax.ppermute(edge_rows[:rim], "dom", backward))
+    )(send, pool.reshape(steps, NT), table, scale, node, edge, ein, eout, nin, nout, bias, gain)
 
 
 def coarse_kernel(
@@ -346,10 +445,10 @@
 ):
     groups = lax.axis_size("group")
     clusters, width = coarse_lat.shape
-    rim = halo_list.shape[0] // 2
-    low, high = exchange(border(node_lat, halo_list), rim)
+    table, scale = front(halo_list, node_lat, fine_edge_in)
+    table = table.reshape(table.shape[0], 1, table.shape[1])
     fine_out, part = fine_level(
-        groups, clusters, edge_send, pool_id, node_lat, low, high, edge_lat,
+        groups, clusters, edge_send, pool_id, table, scale, node_lat, edge_lat,
         fine_edge_in, fine_edge_out, fine_node_in, fine_node_out, fine_bias, fine_gain,
     )
     coarse_out = coarse_level(

time: 57.2 us -> 56.2 us (0.983)
  local copies, waits for them, and re-layouts: 1.05 us -> 13.1 us
  starting transfers between devices: 6.52 us -> 0 us
  waiting for transfers between devices: 5.46 us -> 0 us
  matrix products: 2.83 us -> 0 us
  Pallas kernels: 40.2 us -> 41.8 us
    unnamed x39 -> x53, local copies, waits for them, and re-layouts: 0.75 us -> 11.4 us
    pallas_call x0 -> x1, Pallas kernels: none -> 8.33 us  [front(): pl.pallas_call(front_kernel, in_specs=[pl.BlockSpec(memory_space=pltpu.VM...]
    pallas_call x1, Pallas kernels: 25.8 us -> 17.9 us  [fine_level(): pl.pallas_call(functools.partial(fine_kernel, groups, clusters), grid=(st...]
    ppermute x2 -> x0, starting transfers between devices: 6.52 us -> none  [the longest x1 4.6 us: exchange(): lax.ppermute(edge_rows[rim:], 'dom', forward)]
    ppermute x2 -> x0, waiting for transfers between devices: 5.46 us -> none  [the longest x1 4.4 us: exchange(): lax.ppermute(edge_rows[:rim], 'dom', backward)]
    dot_general x1 -> x0, matrix products: 2.83 us -> none  [dot(): return jnp.dot(a, b, preferred_element_type=F32)]
    pallas_call x1, Pallas kernels: 14.3 us -> 15.6 us  [coarse_level(): pl.pallas_call(coarse_kernel, in_specs=[pl.BlockSpec(memory_space=pltpu.V...]
    reshape x1, local copies, waits for them, and re-layouts: 0.13 us -> 0.82 us  [coarse_level(): send.reshape(rows, DEG)]
  transfers between devices with their start and end apart: 2 -> 0, of which waited for: 2 -> 0; matrix products, arithmetic and copies ran while one was open for 0% -> 0% of each run, Pallas kernels for 0% -> 0%
where the time goes in v3:
time: 56.2 us; the launch traced here: 55.7 us
  Pallas kernels  41.8 us (74%)
  local copies, waits for them, and re-layouts  13.1 us (23%)
  between operations  0.86 us (2%)
    pallas_call x1, Pallas kernels, fine_level(): pl.pallas_call(functools.partial(fine_kernel, groups, clusters), grid=(st...  17.9 us
    pallas_call x1, Pallas kernels, coarse_level(): pl.pallas_call(coarse_kernel, in_specs=[pl.BlockSpec(memory_space=pltpu.V...  15.6 us
    unnamed x53, local copies, waits for them, and re-layouts  11.4 us
    pallas_call x1, Pallas kernels, front(): pl.pallas_call(front_kernel, in_specs=[pl.BlockSpec(memory_space=pltpu.VM...  8.33 us

profile of v3, /device:TPU:1, one launch (start us, length us, event | category | flops | bytes accessed | tf_op | source)
XLA Modules:
  0.0 55.7 jit_solution(5983429705410228067)
XLA Ops:
  0.6 1.2 %copy-done = bf16[2048,256]{1,0:T(8,128)(2,1)S(1)} copy-done((bf16[2048,256]{1,0:T(8,128)(2,1)S(1)}, bf16[2048,256]{1,0:T(8,128)(2,1)}, u32[]{:S(2)}) %copy-start) | copy-done | bytes 1048600
  1.9 1.0 %copy-done.3 = bf16[3,256,256]{2,1,0:T(8,128)(2,1)S(1)} copy-done((bf16[3,256,256]{2,1,0:T(8,128)(2,1)S(1)}, bf16[3,256,256]{2,1,0:T(8,128)(2,1)}, u32[]{:S(2)}) %copy-start.3) | copy-done | bytes 393240
  2.9 0.7 %copy-done.14 = s32[1024]{0:T(1024)S(1)} copy-done((s32[1024]{0:T(1024)S(1)}, s32[1024]{0:T(1024)}, u32[]{:S(2)}) %copy-start.14) | copy-done | bytes 4120
  3.6 0.0 copy-start.8
  3.6 8.3 %front.1 = (s32[3072,128]{1,0:T(8,128)S(1)}, f32[1,256]{1,0:T(1,128)S(1)}) custom-call(s32[8,128]{1,0:T(8,128)S(1)} %bitcast.3, bf16[2048,256]{1,0:T(8,128)(2,1)S(1)} %copy-done, bf16[3,256,256]{2,1,0:T(8,128)(2,1)S(1)} %copy-done.3), custom_call_target="tpu_custom_call" | custom-call | flops 1500000000 | bytes 3000000 | tf_op jit(solution)/shard_map/front/pallas_call | solution.py:144
  11.9 1.2 %copy-done.19 = s32[3072,128]{1,0:T(8,128)} copy-done((s32[3072,128]{1,0:T(8,128)}, s32[3072,128]{1,0:T(8,128)S(1)}, u32[]{:S(2)}) %copy-start.19) | copy-done | bytes 1572888
  13.1 0.6 %copy-done.23 = f32[1,256]{1,0:T(1,128)} copy-done((f32[1,256]{1,0:T(1,128)}, f32[1,256]{1,0:T(1,128)S(1)}, u32[]{:S(2)}) %copy-start.23) | copy-done | bytes 1048
  13.7 0.0 copy-start.13
  13.7 0.7 %copy-done.13 = s32[8192]{0:T(1024)S(1)} copy-done((s32[8192]{0:T(1024)S(1)}, s32[8192]{0:T(1024)}, u32[]{:S(2)}) %copy-start.13) | copy-done | bytes 32792
  14.5 0.7 %copy-done.17 = f32[2,256]{1,0:T(2,128)S(1)} copy-done((f32[2,256]{1,0:T(2,128)S(1)}, f32[2,256]{1,0:T(2,128)}, u32[]{:S(2)}) %copy-start.17) | copy-done | bytes 2072
  15.2 1.4 %copy-done.20 = s32[3072,128]{1,0:T(8,128)S(1)} copy-done((s32[3072,128]{1,0:T(8,128)S(1)}, s32[3072,128]{1,0:T(8,128)}, u32[]{:S(2)}) %copy-start.20) | copy-done | bytes 1572888
  16.6 0.7 %copy-done.24 = f32[1,256]{1,0:T(1,128)S(1)} copy-done((f32[1,256]{1,0:T(1,128)S(1)}, f32[1,256]{1,0:T(1,128)}, u32[]{:S(2)}) %copy-start.24) | copy-done | bytes 1048
  17.3 0.0 copy-start.11
  17.3 0.0 copy-start.12
  17.3 0.0 copy-start.16
  17.3 17.9 %fine_level.1 = (bf16[2048,256]{1,0:T(8,128)(2,1)}, bf16[4,272,256]{2,1,0:T(8,128)(2,1)S(1)}) custom-call(s32[8192]{0:T(1024)S(1)} %copy-done.13, s32[8,256]{1,0:T(8,128)S(1)} %reshape.19.pool, s32[3072,1,128]{2,1,0:T(1,128)S(1)} %bitcast.4, f32[1,256]{1,0:T(1,128)S(1)} %copy-done.24, bf16[2048,256]{1,0:T(8,128)(2,1)S(1)} %copy-done.1, ...), custom_call_target="tpu_custom_call" | custom-call | flops 7000000000 | bytes 9000000 | tf_op jit(solution)/shard_map/fine_level/pallas_call | solution.py:246
  35.2 0.8 %copy-done.21 = bf16[4,272,256]{2,1,0:T(8,128)(2,1)} copy-done((bf16[4,272,256]{2,1,0:T(8,128)(2,1)}, bf16[4,272,256]{2,1,0:T(8,128)(2,1)S(1)}, u32[]{:S(2)}) %copy-start.21) | copy-done | bytes 557080
  36.0 0.8 %copy.23.lists = s32[256,1]{1,0:T(8,128)S(1)} copy(s32[256,1]{0,1:T(1,128)} %bitcast.5) | data formatting | bytes 2048 | tf_op jit(solution)/shard_map/reshape | solution.py:436
  36.8 0.8 %reshape.22.sends = s32[256,4]{1,0:T(8,128)S(1)} reshape(s32[1024]{0:T(1024)} %param.28) | data formatting | bytes 8192 | tf_op jit(solution)/shard_map/reshape | solution.py:436
  37.7 0.0 copy-start.18
  37.7 0.7 %copy-done.18 = f32[2,256]{1,0:T(2,128)S(1)} copy-done((f32[2,256]{1,0:T(2,128)S(1)}, f32[2,256]{1,0:T(2,128)}, u32[]{:S(2)}) %copy-start.18) | copy-done | bytes 2072
  38.4 1.1 %copy-done.22 = bf16[4,272,256]{2,1,0:T(8,128)(2,1)S(1)} copy-done((bf16[4,272,256]{2,1,0:T(8,128)(2,1)S(1)}, bf16[4,272,256]{2,1,0:T(8,128)(2,1)}, u32[]{:S(2)}) %copy-start.22) | copy-done | bytes 557080
  39.4 15.6 %coarse_level.1 = bf16[256,256]{1,0:T(8,128)(2,1)S(1)} custom-call(bf16[4,272,256]{2,1,0:T(8,128)(2,1)S(1)} %copy-done.22, bf16[256,256]{1,0:T(8,128)(2,1)S(1)} %copy-done.10, bf16[1024,256]{1,0:T(8,128)(2,1)S(1)} %copy-done.2, s32[256,4]{1,0:T(8,128)S(1)} %reshape.22.sends, s32[256,1]{1,0:T(8,128)S(1)} %copy.23.lists, bf16[3,256,256]{2,1,0:T(8,128)(2,1)S(1)} %copy-done.5, ...), custom_call_target="tpu_custom_call" | custom-call | flops 1500000000 | bytes 3000000 | tf_op jit(solution)/shard_map/coarse_level/pallas_call | solution.py:414
  55.1 0.7 %copy.25 = bf16[256,256]{1,0:T(8,128)(2,1)} copy(bf16[256,256]{1,0:T(8,128)(2,1)S(1)} %coarse_level.1) | data formatting | bytes 262144
  (35 shorter events, 0.1 us)
Async XLA Ops:
  0.6 1.2 %copy-start = (bf16[2048,256]{1,0:T(8,128)(2,1)S(1)}, bf16[2048,256]{1,0:T(8,128)(2,1)}, u32[]{:S(2)}) copy-start(bf16[2048,256]{1,0:T(8,128)(2,1)} %node.3) | copy-start | bytes 3145732
  1.9 1.0 %copy-start.3 = (bf16[3,256,256]{2,1,0:T(8,128)(2,1)S(1)}, bf16[3,256,256]{2,1,0:T(8,128)(2,1)}, u32[]{:S(2)}) copy-start(bf16[3,256,256]{2,1,0:T(8,128)(2,1)} %ein.4) | copy-start | bytes 1179652
  2.9 0.7 %copy-start.14 = (s32[1024]{0:T(1024)S(1)}, s32[1024]{0:T(1024)}, u32[]{:S(2)}) copy-start(s32[1024]{0:T(1024)} %param.24) | copy-start | bytes 12292
  3.5 10.1 %copy-start.25 = (s32[2048]{0:T(1024)S(1)}, s32[2048]{0:T(1024)}, u32[]{:S(2)}) copy-start(s32[2048]{0:T(1024)} %param.25) | copy-start | bytes 24580
  3.5 10.1 %copy-start.1 = (bf16[2048,256]{1,0:T(8,128)(2,1)S(1)}, bf16[2048,256]{1,0:T(8,128)(2,1)}, u32[]{:S(2)}) copy-start(bf16[2048,256]{1,0:T(8,128)(2,1)} %node.3) | copy-start | bytes 3145732
  3.5 10.1 %copy-start.4 = (bf16[3,256,256]{2,1,0:T(8,128)(2,1)S(1)}, bf16[3,256,256]{2,1,0:T(8,128)(2,1)}, u32[]{:S(2)}) copy-start(bf16[3,256,256]{2,1,0:T(8,128)(2,1)} %ein.4) | copy-start | bytes 1179652
  3.5 10.1 %copy-start.6 = (bf16[2,256,256]{2,1,0:T(8,128)(2,1)S(1)}, bf16[2,256,256]{2,1,0:T(8,128)(2,1)}, u32[]{:S(2)}) copy-start(bf16[2,256,256]{2,1,0:T(8,128)(2,1)} %nin.2) | copy-start | bytes 786436
  3.6 10.1 %copy-start.8 = (bf16[256,256]{1,0:T(8,128)(2,1)S(1)}, bf16[256,256]{1,0:T(8,128)(2,1)}, u32[]{:S(2)}) copy-start(bf16[256,256]{1,0:T(8,128)(2,1)} %eout.2) | copy-start | bytes 393220
  3.6 10.1 %copy-start.9 = (bf16[256,256]{1,0:T(8,128)(2,1)S(1)}, bf16[256,256]{1,0:T(8,128)(2,1)}, u32[]{:S(2)}) copy-start(bf16[256,256]{1,0:T(8,128)(2,1)} %nout.2) | copy-start | bytes 393220
  3.6 10.1 %copy-start.15 = (f32[4,256]{1,0:T(4,128)S(1)}, f32[4,256]{1,0:T(4,128)}, u32[]{:S(2)}) copy-start(f32[4,256]{1,0:T(4,128)} %bias.2) | copy-start | bytes 12292
  11.9 1.2 %copy-start.19 = (s32[3072,128]{1,0:T(8,128)}, s32[3072,128]{1,0:T(8,128)S(1)}, u32[]{:S(2)}) copy-start(s32[3072,128]{1,0:T(8,128)S(1)} %get-tuple-element.6) | copy-start | bytes 4718596
  13.7 0.8 %copy-start.13 = (s32[8192]{0:T(1024)S(1)}, s32[8192]{0:T(1024)}, u32[]{:S(2)}) copy-start(s32[8192]{0:T(1024)} %send.1) | copy-start | bytes 98308
  14.5 0.7 %copy-start.17 = (f32[2,256]{1,0:T(2,128)S(1)}, f32[2,256]{1,0:T(2,128)}, u32[]{:S(2)}) copy-start(f32[2,256]{1,0:T(2,128)} %gain.2) | copy-start | bytes 6148
  15.2 1.4 %copy-start.20 = (s32[3072,128]{1,0:T(8,128)S(1)}, s32[3072,128]{1,0:T(8,128)}, u32[]{:S(2)}) copy-start(s32[3072,128]{1,0:T(8,128)} %copy-done.19) | copy-start | bytes 4718596
  17.3 20.4 %copy-start.2 = (bf16[1024,256]{1,0:T(8,128)(2,1)S(1)}, bf16[1024,256]{1,0:T(8,128)(2,1)}, u32[]{:S(2)}) copy-start(bf16[1024,256]{1,0:T(8,128)(2,1)} %edge.3) | copy-start | bytes 1572868
  17.3 20.4 %copy-start.5 = (bf16[3,256,256]{2,1,0:T(8,128)(2,1)S(1)}, bf16[3,256,256]{2,1,0:T(8,128)(2,1)}, u32[]{:S(2)}) copy-start(bf16[3,256,256]{2,1,0:T(8,128)(2,1)} %ein.5) | copy-start | bytes 1179652
  17.3 20.4 %copy-start.7 = (bf16[2,256,256]{2,1,0:T(8,128)(2,1)S(1)}, bf16[2,256,256]{2,1,0:T(8,128)(2,1)}, u32[]{:S(2)}) copy-start(bf16[2,256,256]{2,1,0:T(8,128)(2,1)} %nin.3) | copy-start | bytes 786436
  17.3 20.4 %copy-start.10 = (bf16[256,256]{1,0:T(8,128)(2,1)S(1)}, bf16[256,256]{1,0:T(8,128)(2,1)}, u32[]{:S(2)}) copy-start(bf16[256,256]{1,0:T(8,128)(2,1)} %lat.1) | copy-start | bytes 393220
  17.3 20.4 %copy-start.11 = (bf16[256,256]{1,0:T(8,128)(2,1)S(1)}, bf16[256,256]{1,0:T(8,128)(2,1)}, u32[]{:S(2)}) copy-start(bf16[256,256]{1,0:T(8,128)(2,1)} %eout.3) | copy-start | bytes 393220
  17.3 20.4 %copy-start.12 = (bf16[256,256]{1,0:T(8,128)(2,1)S(1)}, bf16[256,256]{1,0:T(8,128)(2,1)}, u32[]{:S(2)}) copy-start(bf16[256,256]{1,0:T(8,128)(2,1)} %nout.3) | copy-start | bytes 393220
  17.3 20.4 %copy-start.16 = (f32[4,256]{1,0:T(4,128)S(1)}, f32[4,256]{1,0:T(4,128)}, u32[]{:S(2)}) copy-start(f32[4,256]{1,0:T(4,128)} %bias.3) | copy-start | bytes 12292
  35.2 0.8 %copy-start.21 = (bf16[4,272,256]{2,1,0:T(8,128)(2,1)}, bf16[4,272,256]{2,1,0:T(8,128)(2,1)S(1)}, u32[]{:S(2)}) copy-start(bf16[4,272,256]{2,1,0:T(8,128)(2,1)S(1)} %get-tuple-element.9.part) | copy-start | bytes 1671172
  37.7 0.7 %copy-start.18 = (f32[2,256]{1,0:T(2,128)S(1)}, f32[2,256]{1,0:T(2,128)}, u32[]{:S(2)}) copy-start(f32[2,256]{1,0:T(2,128)} %gain.3) | copy-start | bytes 6148
  38.4 1.1 %copy-start.22 = (bf16[4,272,256]{2,1,0:T(8,128)(2,1)S(1)}, bf16[4,272,256]{2,1,0:T(8,128)(2,1)}, u32[]{:S(2)}) copy-start(bf16[4,272,256]{2,1,0:T(8,128)(2,1)} %copy-done.21) | copy-start | bytes 1671172
  (2 other events, 1.2 us)

commit v4 on v3

--- a/solution.py
+++ b/solution.py
@@ -12,6 +12,7 @@
 BF16 = jnp.bfloat16
 NT = 256
 DEG = 4
+VMEM = 60 * 1024 * 1024
 
 
 def dot(a, b):
@@ -29,6 +30,13 @@
 
 def column(row):
     return jnp.broadcast_to(row, (128, 128)).T
+
+
+def one_hot(names, starts):
+    lane = lax.broadcasted_iota(jnp.int32, names.shape, 1)
+    return jnp.concatenate(
+        [jnp.where(names == lane + j, 1.0, 0.0).astype(BF16) for j in starts], axis=1
+    )
 
 
 def neighbours():
@@ -50,7 +58,7 @@
 
 
 def front_kernel(
-    lists, node, ein, table, scale, proj, rim_out, rim_in, rim_send, rim_recv
+    lists, pool, node, ein, table, scale, count, proj, rim_out, rim_in, rim_send, rim_recv
 ):
     rows, width = node.shape
     rim = rim_in.shape[1]
@@ -84,11 +92,7 @@
     def pick(side):
         for r in range(0, rim, 128):
             at = (side * rim + r) // 128
-            names = column(lists[at:at + 1, :])
-            chosen = jnp.concatenate(
-                [jnp.where(names == lane + j, 1.0, 0.0).astype(BF16) for j in range(0, rows, 128)],
-                axis=1,
-            )
+            chosen = one_hot(column(lists[at:at + 1, :]), range(0, rows, 128))
             rim_out[side, r:r + 128, :] = dot(chosen, node[...]).astype(BF16)
 
     pick(0)
@@ -109,6 +113,18 @@
         p = dot(node[r:r + 256, :], ein[0])
         proj[rim + r:rim + r + 256, :] = p
         top = jnp.maximum(top, jnp.max(jnp.abs(p), axis=0, keepdims=True))
+
+    for c in range(0, count.shape[1], 128):
+        count[:, c:c + 128] = jnp.zeros((1, 128), F32)
+
+    def tally(r, carry):
+        names = column(pool[pl.ds(r, 1), :])
+        for c in range(0, count.shape[1], 128):
+            hit = jnp.where(names == lane + c, 1.0, 0.0)
+            count[:, c:c + 128] += jnp.sum(hit, axis=0, keepdims=True)
+        return carry
+
+    lax.fori_loop(0, rows // 128, tally, 0)
 
     @pl.when(has_high)
     def _():
@@ -138,15 +154,16 @@
         up.wait_send()
 
 
-def front(lists, node, ein):
+def front(columns, lists, pool, node, ein):
     rows, width = node.shape
     rim = lists.shape[0] // 2
     return pl.pallas_call(
         front_kernel,
-        in_specs=[pl.BlockSpec(memory_space=pltpu.VMEM)] * 3,
-        out_specs=[pl.BlockSpec(memory_space=pltpu.VMEM)] * 2,
+        in_specs=[pl.BlockSpec(memory_space=pltpu.VMEM)] * 4,
+        out_specs=[pl.BlockSpec(memory_space=pltpu.VMEM)] * 3,
         out_shape=[jax.ShapeDtypeStruct((rows + 2 * rim, 128), jnp.int32),
-                   jax.ShapeDtypeStruct((1, width), F32)],
+                   jax.ShapeDtypeStruct((1, width), F32),
+                   jax.ShapeDtypeStruct((1, columns), F32)],
         scratch_shapes=[
             pltpu.VMEM((rows + 2 * rim, width), F32),
             pltpu.VMEM((2, rim, width), BF16),
@@ -155,26 +172,23 @@
             pltpu.SemaphoreType.DMA((2,)),
         ],
         compiler_params=pltpu.CompilerParams(
-            vmem_limit_bytes=32 * 1024 * 1024, collective_id=1, has_side_effects=True
+            vmem_limit_bytes=VMEM, collective_id=1, has_side_effects=True
         ),
         cost_estimate=pl.CostEstimate(flops=1_500_000_000, bytes_accessed=3_000_000, transcendentals=0),
         name="front",
-    )(lists.reshape(2 * rim // 128, 128), node, ein)
+    )(lists.reshape(-1, 128), pool.reshape(-1, 128), node, ein)
 
 
 def fine_kernel(
     groups, clusters,
-    send, pool, table, scale, node, edge, ein, eout, nin, nout, bias, gain,
+    send, pool, count, table, scale, node, edge, ein, eout, nin, nout, bias, gain,
     out, part,
-    gath, pre_lo, pre_hi, eoc, noc, bc, acc, cnt,
+    gath, pre_lo, pre_hi, eoc, noc, bc, acc, held,
 ):
     step = pl.program_id(0)
     steps = pl.num_programs(0)
     et = NT * DEG
-
-    def fetch(tile, k, n):
-        at = send[tile * et + n * DEG + k]
-        gath[pl.ds(k * NT + n, 1), :] = table[at]
+    first = step * et
 
     @pl.when(step == 0)
     def _():
@@ -183,23 +197,32 @@
         b = bias[...]
         bc[...] = b - jnp.mean(b, axis=-1, keepdims=True)
         acc[...] = jnp.zeros_like(acc)
-        cnt[...] = jnp.zeros_like(cnt)
-
-        def first(n, carry):
-            for k in range(DEG):
-                fetch(0, k, n)
-            return carry
-
-        lax.fori_loop(0, NT, first, 0, unroll=8)
-
-    nxt = jnp.minimum(step + 1, steps - 1)
+        held[...] = jnp.zeros_like(held)
+
+    def gather(k):
+        for n in range(NT):
+            gath[pl.ds(k * NT + n, 1), :] = table[send[first + (n * DEG + k)]]
+
+    def add_members(tile):
+        ids = jnp.concatenate(
+            [pool[pl.ds(tile * (NT // 128) + j, 1), :] for j in range(NT // 128)], axis=1
+        )
+        rows = held[...]
+        for c in range(0, groups * clusters, 256):
+            names = lax.broadcasted_iota(jnp.int32, (256, NT), 0) + c
+            acc[c:c + 256, :] += dot(jnp.where(names == ids, 1.0, 0.0).astype(BF16), rows)
+
+    gather(0)
     p = dot(edge[...], ein[2])
     pre_lo[...] = p[:, :128]
     pre_hi[...] = p[:, 128:]
     own = node[...]
     rv = dot(own, ein[1]) + bias[0:1, :]
+    add_members(jnp.maximum(step - 1, 0))
     total = jnp.zeros((NT, 256), F32)
     for k in range(DEG):
+        if k + 1 < DEG:
+            gather(k + 1)
         g = gath[k * NT:(k + 1) * NT, :]
         s = jnp.concatenate([(g << 16) >> 16, g >> 16], axis=1).astype(F32) * scale[...]
         e = jnp.concatenate(
@@ -207,38 +230,28 @@
         )
         h = jnp.maximum(e + s + rv, 0.0).astype(BF16)
         total = total + unit_rows(dot(h, eoc[...]) + bc[1:2, :])
-        for n in range(NT):
-            fetch(nxt, k, n)
     summed = (total * gain[0:1, :]).astype(BF16)
     h = jnp.maximum(dot(own, nin[0]) + dot(summed, nin[1]) + bias[2:3, :], 0.0).astype(BF16)
     update = unit_rows(dot(h, noc[...]) + bc[3:4, :]) * gain[1:2, :]
     result = (own.astype(F32) + update).astype(BF16)
     out[...] = result
-    ids = pool[pl.ds(step, 1), :]
-    ones = jnp.ones((16, NT), BF16)
-    for g in range(groups):
-        c = g * clusters
-        names = lax.broadcasted_iota(jnp.int32, (clusters, NT), 0) + c
-        member = jnp.where(names == ids, 1.0, 0.0).astype(BF16)
-        acc[c:c + clusters, :] += dot(member, result)
-        cnt[g] += lax.dot_general(
-            ones, member, (((1,), (1,)), ((), ())), preferred_element_type=F32
-        )
+    held[...] = result
 
     @pl.when(step == steps - 1)
     def _():
+        add_members(step)
         for g in range(groups):
             c = g * clusters
             part[g, 0:clusters, :] = acc[c:c + clusters, :].astype(BF16)
-            n = cnt[g]
+            n = count[:, c:c + clusters]
             big = jnp.floor(n * (1.0 / 256.0)) * 256.0
-            which = lax.broadcasted_iota(jnp.int32, n.shape, 0)
+            which = lax.broadcasted_iota(jnp.int32, (16, clusters), 0)
             part[g, clusters:clusters + 16, :] = jnp.where(
                 which == 0, n - big, jnp.where(which == 1, big, 0.0)
             ).astype(BF16)
 
 
-def fine_level(groups, clusters, send, pool, table, scale, node, edge, ein, eout, nin, nout, bias, gain):
+def fine_level(groups, clusters, send, pool, count, table, scale, node, edge, ein, eout, nin, nout, bias, gain):
     rows, width = node.shape
     steps = rows // NT
     et = NT * DEG
@@ -246,7 +259,7 @@
     return pl.pallas_call(
         functools.partial(fine_kernel, groups, clusters),
         grid=(steps,),
-        in_specs=[pl.BlockSpec(memory_space=pltpu.SMEM), whole, whole, whole,
+        in_specs=[pl.BlockSpec(memory_space=pltpu.SMEM), whole, whole, whole, whole,
                   pl.BlockSpec((NT, width), lambda i: (i, 0)),
                   pl.BlockSpec((et, width), lambda i: (i, 0))] + [whole] * 6,
         out_specs=[pl.BlockSpec((NT, width), lambda i: (i, 0)),
@@ -261,18 +274,18 @@
             pltpu.VMEM((width, width), BF16),
             pltpu.VMEM((4, width), F32),
             pltpu.VMEM((groups * clusters, width), F32),
-            pltpu.VMEM((groups, 16, clusters), F32),
+            pltpu.VMEM((NT, width), BF16),
         ],
-        compiler_params=pltpu.CompilerParams(vmem_limit_bytes=48 * 1024 * 1024),
+        compiler_params=pltpu.CompilerParams(vmem_limit_bytes=VMEM),
         cost_estimate=pl.CostEstimate(flops=7_000_000_000, bytes_accessed=9_000_000, transcendentals=0),
         name="fine_level",
-    )(send, pool.reshape(steps, NT), table, scale, node, edge, ein, eout, nin, nout, bias, gain)
+    )(send, pool.reshape(-1, 128), count, table, scale, node, edge, ein, eout, nin, nout, bias, gain)
 
 
 def coarse_kernel(
     part, lat, edge, sends, lists, ein, eout, nin, nout, bias, gain,
     out,
-    got, edges_lo, edges_hi, rim_out, rim_in, mix, sum_send, sum_recv, rim_send, rim_recv,
+    got, edges_lo, edges_hi, rim_out, rim_in, mix, names, sum_send, sum_recv, rim_send, rim_recv,
 ):
     groups = part.shape[0]
     rows, width = lat.shape
@@ -320,6 +333,8 @@
         p = dot(edge[r:r + 256, :], ein[2])
         edges_lo[r:r + 256, :] = p[:, :128]
         edges_hi[r:r + 256, :] = p[:, 128:]
+    for r in range(sends.shape[0]):
+        names[r * 128:(r + 1) * 128, :] = column(sends[r:r + 1, :])
     sums = part[mine].astype(F32)
     for copy in copies:
         copy.wait_recv()
@@ -329,8 +344,8 @@
     inv = jnp.broadcast_to(1.0 / jnp.maximum(members, 1.0), (128, rows)).T
     inv = jnp.concatenate([inv] * (width // 128), axis=1)
     own = (lat[...].astype(F32) + sums[:rows, :] * inv).astype(BF16)
-    names = lax.broadcasted_iota(jnp.int32, (2 * rim, rows), 1)
-    chosen = jnp.where(names == lists[...], 1.0, 0.0).astype(BF16)
+    picks = jnp.concatenate([column(lists[r:r + 1, :]) for r in range(lists.shape[0])], axis=0)
+    chosen = one_hot(picks, range(0, rows, 128))
     border_rows = dot(chosen, own).astype(BF16)
     rim_out[0] = border_rows[:rim, :]
     rim_out[1] = border_rows[rim:, :]
@@ -364,11 +379,10 @@
     sender = dot(own, ein[0]).astype(BF16)
     recv = dot(own, ein[1]) + b[0:1, :]
     npre = dot(own, nin[0]) + b[2:3, :]
-    inner = lax.broadcasted_iota(jnp.int32, (rows, rows), 1) + rim
-    outer = lax.broadcasted_iota(jnp.int32, (rows, 2 * rim), 1)
-    outer = outer + jnp.where(outer >= rim, rows, 0)
+    inner = range(rim, rim + rows, 128)
+    outer = list(range(0, rim, 128)) + list(range(rim + rows, 2 * rim + rows, 128))
     for k in range(DEG):
-        member = jnp.where(inner == sends[:, k:k + 1], 1.0, 0.0).astype(BF16)
+        member = one_hot(names[pl.ds(k, rows, stride=DEG), :], inner)
         e = jnp.concatenate(
             [edges_lo[pl.ds(k, rows, stride=DEG), :], edges_hi[pl.ds(k, rows, stride=DEG), :]],
             axis=1,
@@ -388,7 +402,7 @@
     rims = jnp.concatenate([low, high], axis=0)
     total = jnp.zeros((rows, width), F32)
     for k in range(DEG):
-        member = jnp.where(outer == sends[:, k:k + 1], 1.0, 0.0).astype(BF16)
+        member = one_hot(names[pl.ds(k, rows, stride=DEG), :], outer)
         h = jnp.maximum(mix[k] + dot(member, rims), 0.0).astype(BF16)
         total = total + unit_rows(dot(h, eoc) + bc[1:2, :])
     summed = (total * gain[0:1, :]).astype(BF16)
@@ -423,17 +437,18 @@
             pltpu.VMEM((2, rim, width), BF16),
             pltpu.VMEM((2, rim, width), BF16),
             pltpu.VMEM((DEG, rows, width), F32),
+            pltpu.VMEM((edge.shape[0], 128), jnp.int32),
             pltpu.SemaphoreType.DMA((groups - 1,)),
             pltpu.SemaphoreType.DMA((groups - 1,)),
             pltpu.SemaphoreType.DMA((2,)),
             pltpu.SemaphoreType.DMA((2,)),
         ],
         compiler_params=pltpu.CompilerParams(
-            vmem_limit_bytes=32 * 1024 * 1024, collective_id=0, has_side_effects=True
+            vmem_limit_bytes=VMEM, collective_id=0, has_side_effects=True
         ),
         cost_estimate=pl.CostEstimate(flops=1_500_000_000, bytes_accessed=3_000_000, transcendentals=0),
         name="coarse_level",
-    )(part, lat, edge, send.reshape(rows, DEG), lists.reshape(2 * rim, 1),
+    )(part, lat, edge, send.reshape(-1, 128), lists.reshape(-1, 128),
       ein, eout, nin, nout, bias, gain)
 
 
@@ -445,10 +460,10 @@
 ):
     groups = lax.axis_size("group")
     clusters, width = coarse_lat.shape
-    table, scale = front(halo_list, node_lat, fine_edge_in)
+    table, scale, count = front(groups * clusters, halo_list, pool_id, node_lat, fine_edge_in)
     table = table.reshape(table.shape[0], 1, table.shape[1])
     fine_out, part = fine_level(
-        groups, clusters, edge_send, pool_id, table, scale, node_lat, edge_lat,
+        groups, clusters, edge_send, pool_id, count, table, scale, node_lat, edge_lat,
         fine_edge_in, fine_edge_out, fine_node_in, fine_node_out, fine_bias, fine_gain,
     )
     coarse_out = coarse_level(

time: 56.2 us -> 50 us (0.89)
  local copies, waits for them, and re-layouts: 13.1 us -> 1.57 us
  Pallas kernels: 41.8 us -> 47.6 us
    unnamed x53 -> x1, local copies, waits for them, and re-layouts: 11.4 us -> 1.57 us
    pallas_call x1, Pallas kernels: 8.33 us -> 10.8 us  [front(): pl.pallas_call(front_kernel, in_specs=[pl.BlockSpec(memory_space=pltpu.VM...]
    pallas_call x1, Pallas kernels: 15.6 us -> 17.9 us  [coarse_level(): pl.pallas_call(coarse_kernel, in_specs=[pl.BlockSpec(memory_space=pltpu.V...]
    reshape x3 -> x0, local copies, waits for them, and re-layouts: 1.63 us -> none  [the longest x1 0.82 us: coarse_level(): send.reshape(rows, DEG)]
    pallas_call x1, Pallas kernels: 17.9 us -> 18.8 us  [fine_level(): pl.pallas_call(functools.partial(fine_kernel, groups, clusters), grid=(st...]
where the time goes in v4:
time: 50 us; the launch traced here: 49.8 us
  Pallas kernels  47.6 us (95%)
  local copies, waits for them, and re-layouts  1.57 us (3%)
  between operations  0.65 us (1%)
    pallas_call x1, Pallas kernels, fine_level(): pl.pallas_call(functools.partial(fine_kernel, groups, clusters), grid=(st...  18.8 us
    pallas_call x1, Pallas kernels, coarse_level(): pl.pallas_call(coarse_kernel, in_specs=[pl.BlockSpec(memory_space=pltpu.V...  17.9 us
    pallas_call x1, Pallas kernels, front(): pl.pallas_call(front_kernel, in_specs=[pl.BlockSpec(memory_space=pltpu.VM...  10.8 us
    unnamed x1, local copies, waits for them, and re-layouts  1.57 us

profile of v4, /device:TPU:1, one launch (start us, length us, event | category | flops | bytes accessed | tf_op | source)
XLA Modules:
  0.0 49.8 jit_solution(16179971981490548802)
XLA Ops:
  0.6 10.8 %front.1 = (s32[3072,128]{1,0:T(8,128)}, f32[1,256]{1,0:T(1,128)}, f32[1,1024]{1,0:T(1,128)}) custom-call(s32[8,128]{1,0:T(8,128)} %bitcast.7, s32[16,128]{1,0:T(8,128)} %bitcast.5, bf16[2048,256]{1,0:T(8,128)(2,1)} %node.3, bf16[3,256,256]{2,1,0:T(8,128)(2,1)} %ein.4), custom_call_target="tpu_custom_call" | custom-call | flops 1500000000 | bytes 3000000 | tf_op jit(solution)/shard_map/front/pallas_call | solution.py:160
  11.5 18.8 %fine_level.1 = (bf16[2048,256]{1,0:T(8,128)(2,1)}, bf16[4,272,256]{2,1,0:T(8,128)(2,1)}) custom-call(s32[8192]{0:T(1024)} %send.1, s32[16,128]{1,0:T(8,128)} %bitcast.6, f32[1,1024]{1,0:T(1,128)} %get-tuple-element.7.count, s32[3072,1,128]{2,1,0:T(1,128)} %bitcast.10, f32[1,256]{1,0:T(1,128)} %get-tuple-element.9.scale, bf16[2048,256]{1,0:T(8,128)(2,1)} %node.3, ...), custom_call_target="tpu_custom_call" | custom-call | flops 7000000000 | bytes 9000000 | tf_op jit(solution)/shard_map/fine_level/pallas_call | solution.py:259
  30.3 17.9 %coarse_level.1 = bf16[256,256]{1,0:T(8,128)(2,1)} custom-call(bf16[4,272,256]{2,1,0:T(8,128)(2,1)} %get-tuple-element.11.part, bf16[256,256]{1,0:T(8,128)(2,1)} %lat.1, bf16[1024,256]{1,0:T(8,128)(2,1)} %edge.3, s32[8,128]{1,0:T(8,128)} %bitcast.8, s32[2,128]{1,0:T(2,128)} %bitcast.9, bf16[3,256,256]{2,1,0:T(8,128)(2,1)} %ein.5, bf16[256,256]{1,0:T(8,128)(2,1)} %eout.3, ...), custom_call_target="tpu_custom_call" | custom-call | flops 1500000000 | bytes 3000000 | tf_op jit(solution)/shard_map/coarse_level/pallas_call | solution.py:428
  48.3 1.6 %copy.24 = bf16[256,256]{1,0:T(8,128)(2,1)} copy(bf16[256,256]{1,0:T(8,128)(2,1)} %coarse_level.1) | data formatting | bytes 262144

commit v5 on v4

--- a/solution.py
+++ b/solution.py
@@ -12,6 +12,8 @@
 BF16 = jnp.bfloat16
 NT = 256
 DEG = 4
+BATCH = 16
+PIECES = 2
 VMEM = 60 * 1024 * 1024
 
 
@@ -47,14 +49,19 @@
 
 def rim_copies(rim_out, rim_in, rim_send, rim_recv, below, above):
     mine = lax.axis_index("group")
-    return tuple(
-        pltpu.make_async_remote_copy(
-            src_ref=rim_out.at[i], dst_ref=rim_in.at[1 - i],
-            send_sem=rim_send.at[i], recv_sem=rim_recv.at[i],
-            device_id=(mine, to), device_id_type=pl.DeviceIdType.MESH,
-        )
+    size = rim_out.shape[1] // PIECES
+    return [
+        [
+            pltpu.make_async_remote_copy(
+                src_ref=rim_out.at[i, pl.ds(p * size, size)],
+                dst_ref=rim_in.at[1 - i, pl.ds(p * size, size)],
+                send_sem=rim_send.at[i, p], recv_sem=rim_recv.at[i, p],
+                device_id=(mine, to), device_id_type=pl.DeviceIdType.MESH,
+            )
+            for p in range(PIECES)
+        ]
         for i, to in enumerate((below, above))
-    )
+    ]
 
 
 def front_kernel(
@@ -89,24 +96,29 @@
     down, up = rim_copies(rim_out, rim_in, rim_send, rim_recv, below, above)
     lane = lax.broadcasted_iota(jnp.int32, (128, 128), 1)
 
-    def pick(side):
-        for r in range(0, rim, 128):
+    size = rim // PIECES
+
+    def pick(side, piece):
+        for r in range(piece * size, (piece + 1) * size, 128):
             at = (side * rim + r) // 128
             chosen = one_hot(column(lists[at:at + 1, :]), range(0, rows, 128))
             rim_out[side, r:r + 128, :] = dot(chosen, node[...]).astype(BF16)
 
-    pick(0)
+    pick(0, 0)
     pl.semaphore_wait(barrier, has_low.astype(jnp.int32) + has_high.astype(jnp.int32))
-
-    @pl.when(has_low)
-    def _():
-        down.start()
-
-    pick(1)
-
-    @pl.when(has_high)
-    def _():
-        up.start()
+    for piece in range(PIECES):
+        if piece:
+            pick(0, piece)
+
+        @pl.when(has_low)
+        def _():
+            down[piece].start()
+
+        pick(1, piece)
+
+        @pl.when(has_high)
+        def _():
+            up[piece].start()
 
     top = jnp.full((1, width), 1e-20, F32)
     for r in range(0, rows, 256):
@@ -126,32 +138,32 @@
 
     lax.fori_loop(0, rows // 128, tally, 0)
 
-    @pl.when(has_high)
-    def _():
-        down.wait_recv()
-
-    @pl.when(has_low)
-    def _():
-        up.wait_recv()
-
-    for side, start in ((0, 0), (1, rim + rows)):
-        for r in range(0, rim, 256):
-            p = dot(rim_in[side, r:r + 256, :], ein[0])
-            proj[start + r:start + r + 256, :] = p
-            top = jnp.maximum(top, jnp.max(jnp.abs(p), axis=0, keepdims=True))
+    for piece in range(PIECES):
+        for side, start, there, copies in ((1, rim + rows, has_high, down), (0, 0, has_low, up)):
+
+            @pl.when(there)
+            def _():
+                copies[piece].wait_recv()
+
+            for r in range(piece * size, (piece + 1) * size, 256):
+                p = dot(rim_in[side, r:r + 256, :], ein[0])
+                proj[start + r:start + r + 256, :] = p
+                top = jnp.maximum(top, jnp.max(jnp.abs(p), axis=0, keepdims=True))
     scale[...] = top * (1.0 / 32767.0)
     inv = 32767.0 / top
     for r in range(0, rows + 2 * rim, 256):
         q = jnp.round(proj[r:r + 256, :] * inv).astype(jnp.int32)
         table[r:r + 256, :] = (q[:, :128] & 0xFFFF) | (q[:, 128:] << 16)
 
-    @pl.when(has_low)
-    def _():
-        down.wait_send()
-
-    @pl.when(has_high)
-    def _():
-        up.wait_send()
+    for piece in range(PIECES):
+
+        @pl.when(has_low)
+        def _():
+            down[piece].wait_send()
+
+        @pl.when(has_high)
+        def _():
+            up[piece].wait_send()
 
 
 def front(columns, lists, pool, node, ein):
@@ -168,8 +180,8 @@
             pltpu.VMEM((rows + 2 * rim, width), F32),
             pltpu.VMEM((2, rim, width), BF16),
             pltpu.VMEM((2, rim, width), BF16),
-            pltpu.SemaphoreType.DMA((2,)),
-            pltpu.SemaphoreType.DMA((2,)),
+            pltpu.SemaphoreType.DMA((2, PIECES)),
+            pltpu.SemaphoreType.DMA((2, PIECES)),
         ],
         compiler_params=pltpu.CompilerParams(
             vmem_limit_bytes=VMEM, collective_id=1, has_side_effects=True
@@ -200,8 +212,10 @@
         held[...] = jnp.zeros_like(held)
 
     def gather(k):
-        for n in range(NT):
-            gath[pl.ds(k * NT + n, 1), :] = table[send[first + (n * DEG + k)]]
+        for n in range(0, NT, BATCH):
+            got = [table[send[first + ((n + j) * DEG + k)]] for j in range(BATCH)]
+            for j in range(BATCH):
+                gath[pl.ds(k * NT + n + j, 1), :] = got[j]
 
     def add_members(tile):
         ids = jnp.concatenate(
@@ -285,7 +299,7 @@
 def coarse_kernel(
     part, lat, edge, sends, lists, ein, eout, nin, nout, bias, gain,
     out,
-    got, edges_lo, edges_hi, rim_out, rim_in, mix, names, sum_send, sum_recv, rim_send, rim_recv,
+    got, edges_lo, edges_hi, rim_out, rim_in, mix, names, near, far, chosen, sum_send, sum_recv, rim_send, rim_recv,
 ):
     groups = part.shape[0]
     rows, width = lat.shape
@@ -335,6 +349,14 @@
         edges_hi[r:r + 256, :] = p[:, 128:]
     for r in range(sends.shape[0]):
         names[r * 128:(r + 1) * 128, :] = column(sends[r:r + 1, :])
+    for k in range(DEG):
+        at = names[pl.ds(k, rows, stride=DEG), :]
+        near[k] = one_hot(at, range(rim, rim + rows, 128))
+        far[k] = one_hot(
+            at, list(range(0, rim, 128)) + list(range(rim + rows, 2 * rim + rows, 128))
+        )
+    picks = jnp.concatenate([column(lists[r:r + 1, :]) for r in range(lists.shape[0])], axis=0)
+    chosen[...] = one_hot(picks, range(0, rows, 128))
     sums = part[mine].astype(F32)
     for copy in copies:
         copy.wait_recv()
@@ -344,9 +366,7 @@
     inv = jnp.broadcast_to(1.0 / jnp.maximum(members, 1.0), (128, rows)).T
     inv = jnp.concatenate([inv] * (width // 128), axis=1)
     own = (lat[...].astype(F32) + sums[:rows, :] * inv).astype(BF16)
-    picks = jnp.concatenate([column(lists[r:r + 1, :]) for r in range(lists.shape[0])], axis=0)
-    chosen = one_hot(picks, range(0, rows, 128))
-    border_rows = dot(chosen, own).astype(BF16)
+    border_rows = dot(chosen[...], own).astype(BF16)
     rim_out[0] = border_rows[:rim, :]
     rim_out[1] = border_rows[rim:, :]
     down = pltpu.make_async_remote_copy(
@@ -379,15 +399,12 @@
     sender = dot(own, ein[0]).astype(BF16)
     recv = dot(own, ein[1]) + b[0:1, :]
     npre = dot(own, nin[0]) + b[2:3, :]
-    inner = range(rim, rim + rows, 128)
-    outer = list(range(0, rim, 128)) + list(range(rim + rows, 2 * rim + rows, 128))
     for k in range(DEG):
-        member = one_hot(names[pl.ds(k, rows, stride=DEG), :], inner)
         e = jnp.concatenate(
             [edges_lo[pl.ds(k, rows, stride=DEG), :], edges_hi[pl.ds(k, rows, stride=DEG), :]],
             axis=1,
         )
-        mix[k] = e + recv + dot(member, sender)
+        mix[k] = e + recv + dot(near[k], sender)
 
     @pl.when(has_high)
     def _():
@@ -402,13 +419,12 @@
     rims = jnp.concatenate([low, high], axis=0)
     total = jnp.zeros((rows, width), F32)
     for k in range(DEG):
-        member = one_hot(names[pl.ds(k, rows, stride=DEG), :], outer)
-        h = jnp.maximum(mix[k] + dot(member, rims), 0.0).astype(BF16)
+        h = jnp.maximum(mix[k] + dot(far[k], rims), 0.0).astype(BF16)
         total = total + unit_rows(dot(h, eoc) + bc[1:2, :])
     summed = (total * gain[0:1, :]).astype(BF16)
     h = jnp.maximum(npre + dot(summed, nin[1]), 0.0).astype(BF16)
     update = unit_rows(dot(h, noc) + bc[3:4, :]) * gain[1:2, :]
-    out[...] = (own.astype(F32) + update).astype(BF16)
+    out[...] = own.astype(F32) + update
     for copy in copies:
         copy.wait_send()
 
@@ -429,7 +445,7 @@
         coarse_kernel,
         in_specs=[pl.BlockSpec(memory_space=pltpu.VMEM)] * 11,
         out_specs=pl.BlockSpec(memory_space=pltpu.VMEM),
-        out_shape=jax.ShapeDtypeStruct((rows, width), BF16),
+        out_shape=jax.ShapeDtypeStruct((rows, width), F32),
         scratch_shapes=[
             pltpu.VMEM((groups - 1,) + part.shape[1:], BF16),
             pltpu.VMEM((edge.shape[0], 128), F32),
@@ -438,6 +454,9 @@
             pltpu.VMEM((2, rim, width), BF16),
             pltpu.VMEM((DEG, rows, width), F32),
             pltpu.VMEM((edge.shape[0], 128), jnp.int32),
+            pltpu.VMEM((DEG, rows, rows), BF16),
+            pltpu.VMEM((DEG, rows, 2 * rim), BF16),
+            pltpu.VMEM((2 * rim, rows), BF16),
             pltpu.SemaphoreType.DMA((groups - 1,)),
             pltpu.SemaphoreType.DMA((groups - 1,)),
             pltpu.SemaphoreType.DMA((2,)),
@@ -470,7 +489,7 @@
         part, coarse_lat, cedge_lat, cedge_send, chalo_list,
         coarse_edge_in, coarse_edge_out, coarse_node_in, coarse_node_out, coarse_bias, coarse_gain,
     )
-    return (fine_out, coarse_out)
+    return (fine_out, coarse_out.astype(BF16))
 
 
 def solution(mesh):

time: 50 us -> 49.8 us (level)
  other arithmetic: 0 us -> 1.62 us
  local copies, waits for them, and re-layouts: 1.57 us -> 0 us
    convert_element_type x0 -> x1, other arithmetic: none -> 1.62 us  [body(): return (fine_out, coarse_out.astype(BF16))]
    unnamed x1 -> x0, local copies, waits for them, and re-layouts: 1.57 us -> none
where the time goes in v5:
time: 49.8 us; the launch traced here: 49.6 us
  Pallas kernels  47.3 us (95%)
  other arithmetic  1.62 us (3%)
  between operations  0.65 us (1%)
    pallas_call x1, Pallas kernels, fine_level(): pl.pallas_call(functools.partial(fine_kernel, groups, clusters), grid=(st...  18.9 us
    pallas_call x1, Pallas kernels, coarse_level(): pl.pallas_call(coarse_kernel, in_specs=[pl.BlockSpec(memory_space=pltpu.V...  17.7 us
    pallas_call x1, Pallas kernels, front(): pl.pallas_call(front_kernel, in_specs=[pl.BlockSpec(memory_space=pltpu.VM...  10.7 us
    convert_element_type x1, other arithmetic, body(): return (fine_out, coarse_out.astype(BF16))  1.62 us

profile of v5, /device:TPU:1, one launch (start us, length us, event | category | flops | bytes accessed | tf_op | source)
XLA Modules:
  0.0 49.6 jit_solution(2146496639620668117)
XLA Ops:
  0.6 10.7 %front.1 = (s32[3072,128]{1,0:T(8,128)}, f32[1,256]{1,0:T(1,128)}, f32[1,1024]{1,0:T(1,128)}) custom-call(s32[8,128]{1,0:T(8,128)} %bitcast.7, s32[16,128]{1,0:T(8,128)} %bitcast.5, bf16[2048,256]{1,0:T(8,128)(2,1)} %node.3, bf16[3,256,256]{2,1,0:T(8,128)(2,1)} %ein.4), custom_call_target="tpu_custom_call" | custom-call | flops 1500000000 | bytes 3000000 | tf_op jit(solution)/shard_map/front/pallas_call | solution.py:172
  11.4 18.9 %fine_level.1 = (bf16[2048,256]{1,0:T(8,128)(2,1)}, bf16[4,272,256]{2,1,0:T(8,128)(2,1)}) custom-call(s32[8192]{0:T(1024)} %send.1, s32[16,128]{1,0:T(8,128)} %bitcast.6, f32[1,1024]{1,0:T(1,128)} %get-tuple-element.7.count, s32[3072,1,128]{2,1,0:T(1,128)} %bitcast.10, f32[1,256]{1,0:T(1,128)} %get-tuple-element.9.scale, bf16[2048,256]{1,0:T(8,128)(2,1)} %node.3, ...), custom_call_target="tpu_custom_call" | custom-call | flops 7000000000 | bytes 9000000 | tf_op jit(solution)/shard_map/fine_level/pallas_call | solution.py:273
  30.2 17.7 %coarse_level.1 = f32[256,256]{1,0:T(8,128)} custom-call(bf16[4,272,256]{2,1,0:T(8,128)(2,1)} %get-tuple-element.11.part, bf16[256,256]{1,0:T(8,128)(2,1)} %lat.1, bf16[1024,256]{1,0:T(8,128)(2,1)} %edge.3, s32[8,128]{1,0:T(8,128)} %bitcast.8, s32[2,128]{1,0:T(2,128)} %bitcast.9, bf16[3,256,256]{2,1,0:T(8,128)(2,1)} %ein.5, bf16[256,256]{1,0:T(8,128)(2,1)} %eout.3, ...), custom_call_target="tpu_custom_call" | custom-call | flops 1500000000 | bytes 3000000 | tf_op jit(solution)/shard_map/coarse_level/pallas_call | solution.py:444
  48.0 1.6 %convert_element_type.3 = bf16[256,256]{1,0:T(8,128)(2,1)} convert(f32[256,256]{1,0:T(8,128)} %coarse_level.1) | non-fusion elementwise | flops 65536 | bytes 393216 | tf_op jit(solution)/shard_map/convert_element_type | solution.py:492

commit v6 on v5

--- a/solution.py
+++ b/solution.py
@@ -27,7 +27,10 @@
 
 
 def unit_rows(z):
-    return z * lax.rsqrt(jnp.mean(z * z, axis=-1, keepdims=True) + EPSILON)
+    width = z.shape[1]
+    ones = jnp.full((width, 128), 1.0, BF16)
+    square = dot((z * z).astype(BF16), ones) * (1.0 / width)
+    return z * jnp.concatenate([lax.rsqrt(square + EPSILON)] * (width // 128), axis=1)
 
 
 def column(row):
@@ -297,8 +300,9 @@
 
 
 def coarse_kernel(
-    part, lat, edge, sends, lists, ein, eout, nin, nout, bias, gain,
+    part, lat_far, edge_far, sends, lists, ein_far, eout_far, nin_far, nout_far, bias, gain,
     out,
+    mine_part, lat, edge, ein, eout, nin, nout, local,
     got, edges_lo, edges_hi, rim_out, rim_in, mix, names, near, far, chosen, sum_send, sum_recv, rim_send, rim_recv,
 ):
     groups = part.shape[0]
@@ -327,6 +331,15 @@
     def _():
         pl.semaphore_signal(barrier, inc=1, device_id=(mine, above), device_id_type=mesh_id)
 
+    loads = [
+        pltpu.make_async_copy(source, target, local.at[i])
+        for i, (source, target) in enumerate((
+            (eout_far, eout), (nout_far, nout), (edge_far, edge), (ein_far, ein),
+            (part.at[mine], mine_part), (lat_far, lat), (nin_far, nin),
+        ))
+    ]
+    for load in loads:
+        load.start()
     pl.semaphore_wait(barrier, groups - 1 + has_low.astype(jnp.int32) + has_high.astype(jnp.int32))
     copies = []
     for o in range(1, groups):
@@ -339,6 +352,8 @@
         copy.start()
         copies.append(copy)
 
+    for load in loads:
+        load.wait()
     eoc = centre(eout[...])
     noc = centre(nout[...])
     b = bias[...]
@@ -357,7 +372,7 @@
         )
     picks = jnp.concatenate([column(lists[r:r + 1, :]) for r in range(lists.shape[0])], axis=0)
     chosen[...] = one_hot(picks, range(0, rows, 128))
-    sums = part[mine].astype(F32)
+    sums = mine_part[...].astype(F32)
     for copy in copies:
         copy.wait_recv()
     for o in range(1, groups):
@@ -441,12 +456,22 @@
     groups = part.shape[0]
     rows, width = lat.shape
     rim = lists.shape[0] // 2
+    far = pl.BlockSpec(memory_space=pl.ANY)
+    near = pl.BlockSpec(memory_space=pltpu.VMEM)
     return pl.pallas_call(
         coarse_kernel,
-        in_specs=[pl.BlockSpec(memory_space=pltpu.VMEM)] * 11,
+        in_specs=[far, far, far, near, near, far, far, far, far, near, near],
         out_specs=pl.BlockSpec(memory_space=pltpu.VMEM),
         out_shape=jax.ShapeDtypeStruct((rows, width), F32),
         scratch_shapes=[
+            pltpu.VMEM(part.shape[1:], BF16),
+            pltpu.VMEM(lat.shape, BF16),
+            pltpu.VMEM(edge.shape, BF16),
+            pltpu.VMEM(ein.shape, BF16),
+            pltpu.VMEM(eout.shape, BF16),
+            pltpu.VMEM(nin.shape, BF16),
+            pltpu.VMEM(nout.shape, BF16),
+            pltpu.SemaphoreType.DMA((7,)),
             pltpu.VMEM((groups - 1,) + part.shape[1:], BF16),
             pltpu.VMEM((edge.shape[0], 128), F32),
             pltpu.VMEM((edge.shape[0], 128), F32),

time: 49.8 us -> 50.1 us (level)
    pallas_call x1, Pallas kernels: 18.9 us -> 19.6 us  [fine_level(): pl.pallas_call(functools.partial(fine_kernel, groups, clusters), grid=(st...]
where the time goes in v6:
time: 50.1 us; the launch traced here: 49.9 us
  Pallas kernels  47.6 us (95%)
  other arithmetic  1.62 us (3%)
  between operations  0.65 us (1%)
    pallas_call x1, Pallas kernels, fine_level(): pl.pallas_call(functools.partial(fine_kernel, groups, clusters), grid=(st...  19.6 us
    pallas_call x1, Pallas kernels, coarse_level(): pl.pallas_call(coarse_kernel, in_specs=[far, far, far, near, near, far, f...  17.3 us
    pallas_call x1, Pallas kernels, front(): pl.pallas_call(front_kernel, in_specs=[pl.BlockSpec(memory_space=pltpu.VM...  10.7 us
    convert_element_type x1, other arithmetic, body(): return (fine_out, coarse_out.astype(BF16))  1.62 us

profile of v6, /device:TPU:1, one launch (start us, length us, event | category | flops | bytes accessed | tf_op | source)
XLA Modules:
  0.0 49.9 jit_solution(10974604691396844597)
XLA Ops:
  0.6 10.7 %front.1 = (s32[3072,128]{1,0:T(8,128)}, f32[1,256]{1,0:T(1,128)}, f32[1,1024]{1,0:T(1,128)}) custom-call(s32[8,128]{1,0:T(8,128)} %bitcast.7, s32[16,128]{1,0:T(8,128)} %bitcast.5, bf16[2048,256]{1,0:T(8,128)(2,1)} %node.3, bf16[3,256,256]{2,1,0:T(8,128)(2,1)} %ein.3), custom_call_target="tpu_custom_call" | custom-call | flops 1500000000 | bytes 3000000 | tf_op jit(solution)/shard_map/front/pallas_call | solution.py:175
  11.4 19.6 %fine_level.1 = (bf16[2048,256]{1,0:T(8,128)(2,1)}, bf16[4,272,256]{2,1,0:T(8,128)(2,1)}) custom-call(s32[8192]{0:T(1024)} %send.1, s32[16,128]{1,0:T(8,128)} %bitcast.6, f32[1,1024]{1,0:T(1,128)} %get-tuple-element.7.count, s32[3072,1,128]{2,1,0:T(1,128)} %bitcast.10, f32[1,256]{1,0:T(1,128)} %get-tuple-element.9.scale, bf16[2048,256]{1,0:T(8,128)(2,1)} %node.3, ...), custom_call_target="tpu_custom_call" | custom-call | flops 7000000000 | bytes 9000000 | tf_op jit(solution)/shard_map/fine_level/pallas_call | solution.py:276
  31.0 17.3 %coarse_level.1 = f32[256,256]{1,0:T(8,128)} custom-call(bf16[4,272,256]{2,1,0:T(8,128)(2,1)} %get-tuple-element.11.part, bf16[256,256]{1,0:T(8,128)(2,1)} %lat_far.1, bf16[1024,256]{1,0:T(8,128)(2,1)} %edge_far.1, s32[8,128]{1,0:T(8,128)} %bitcast.8, s32[2,128]{1,0:T(2,128)} %bitcast.9, bf16[3,256,256]{2,1,0:T(8,128)(2,1)} %ein_far.1, ...), custom_call_target="tpu_custom_call" | custom-call | flops 1500000000 | bytes 3000000 | tf_op jit(solution)/shard_map/coarse_level/pallas_call | solution.py:461
  48.2 1.6 %convert_element_type.3 = bf16[256,256]{1,0:T(8,128)(2,1)} convert(f32[256,256]{1,0:T(8,128)} %coarse_level.1) | non-fusion elementwise | flops 65536 | bytes 393216 | tf_op jit(solution)/shard_map/convert_element_type | solution.py:517
